TPU v7x, 256 devices: a whole 4x4x8 slice. The times are simulated.
256 devices in a mesh: dp: 2 (over core), section: 8 (over z), et: 16 (over y, x).
Axes of the slice: x: 4, y: 4, z: 8, core: 2. Of those that a mesh axis runs over, the one named last changes fastest.
Arguments:
- acts: bfloat16 [16, 2, 1024, 4096], P(('dp', 'section'), None, 'et'), parts along dimension 0, may hold values from -6 to 6
- expert_ids: int32 [16, 2, 1024, 1], P(('dp', 'section'), None, 'et'), parts along dimension 0, may hold values from 0 to 3; in each aligned block of 64 rows (0 to 63, 64 to 127, ..., all dimensions but the last counted through in order) at most 24 rows name the same one
- gates: float32 [16, 2, 1024], P(('dp', 'section'), None, 'et'), parts along dimension 0, may hold values from 0.3 to 1
- norm_gain: float32 [16, 4096], P(('dp', 'section')), parts along dimension 0, may hold values from 0.5 to 1.5
- w_gate_up: bfloat16 [16, 16, 4096, 2, 384], P(('dp', 'section'), 'et'), parts along dimension 0, may hold values from -0.09375 to 0.09375
- w_down: bfloat16 [16, 16, 384, 4096], P(('dp', 'section'), 'et'), parts along dimension 0, may hold values from -0.15625 to 0.15625
Outputs:
- layer_out: bfloat16 [16, 2, 1024, 4096], P(('dp', 'section'), None, 'et'), parts along dimension 0
There are 2 independent parts, one for each index of `dp`. A program takes and returns all parts, laid end to end along the dimension named above; each array names one. Nothing has to cross between parts.
Inputs may be any that keep to these rules, and one draw needn't show every extreme that they name: `expert_ids`: in each micro-batch, the 64 tokens of one device name one expert at most 24 times, and some device's tokens name some expert exactly 24 times.
All inputs are finite; a program needn't handle non-finite values.
Results may differ from a plain program's by a relative error of at most 0.0085.
Values may be sent and summed in bfloat16 or wider, within the bound.
No kernel may reach another device: no remote copies, remote signals or barrier semaphores. Data moves between devices by JAX's collectives and lax.ppermute only.
A program may use at most 128 MiB of HBM per device.

v0:
```python
import jax
import jax.numpy as jnp
from jax import lax
from jax.sharding import PartitionSpec as P

QUARTERS = 4


def passed_along(shard, axis, by):
    size = lax.axis_size(axis)
    return lax.ppermute(shard, axis, [(i, (i + by) % size) for i in range(size)])


def normalize(rows, gain):
    values = rows.astype(jnp.float32)
    scale = lax.rsqrt(jnp.mean(values * values, axis=-1, keepdims=True) + 1e-06)
    return (values * scale * gain).astype(jnp.bfloat16)


def expert_rows(buffer, gate_up_w, down_w):
    both = jnp.einsum("rd,dkf->rkf", buffer, gate_up_w, preferred_element_type=jnp.float32)
    hidden = (jax.nn.silu(both[:, 0]) * both[:, 1]).astype(jnp.bfloat16)
    return jnp.dot(hidden, down_w, preferred_element_type=jnp.float32).astype(jnp.bfloat16)


def per_device(acts, expert_ids, gates, norm_gain, w_gate_up, w_down):
    arriving = passed_along(acts, "section", 1)
    local = arriving[0]
    batches, tok_rows, width = local.shape
    normed = normalize(local.reshape(-1, width), norm_gain[0]).reshape(local.shape)
    chosen = expert_ids[0, :, :, 0]
    gate_up_w = w_gate_up[0, 0]
    down_w = w_down[0, 0]
    group = lax.axis_size("et")
    experts = group // QUARTERS
    capacity = min(tok_rows, 3 * tok_rows // (2 * experts))
    whole, whole_ids = (
        lax.all_gather(normed, "et", axis=1, tiled=True),
        lax.all_gather(chosen.astype(jnp.bfloat16), "et", axis=1, tiled=True),
    )
    whole_ids = whole_ids.astype(jnp.int32)
    own_expert = lax.axis_index("et") // QUARTERS
    blocks = whole_ids.reshape(batches, group, tok_rows)
    matches = (blocks == own_expert).astype(jnp.int32)
    slot_rank = jnp.cumsum(matches, axis=2) - 1
    batch_base = jnp.arange(batches, dtype=jnp.int32)[:, None, None] * (group * capacity)
    source_base = jnp.arange(group, dtype=jnp.int32)[None, :, None] * capacity
    slot_total = batches * group * capacity
    slot_index = jnp.where(matches == 1, batch_base + source_base + slot_rank, slot_total).reshape(
        -1
    )
    buffer = (
        jnp.zeros((slot_total + 1, width), jnp.bfloat16)
        .at[slot_index]
        .set(whole.reshape(-1, width))[:slot_total]
    )
    computed = expert_rows(buffer, gate_up_w, down_w)
    padded = jnp.concatenate([computed, jnp.zeros((1, width), jnp.bfloat16)], axis=0)
    terms = padded[slot_index].astype(jnp.float32).reshape(batches, group * tok_rows, width)
    sums = lax.psum_scatter(
        terms.astype(jnp.bfloat16), "et", scatter_dimension=1, tiled=True
    ).astype(jnp.float32)
    result = (local.astype(jnp.float32) + gates[0][:, :, None] * sums).astype(jnp.bfloat16)
    return result[None]


def solution(mesh):
    in_specs = (
        P(("dp", "section"), None, "et", None),
        P(("dp", "section"), None, "et", None),
        P(("dp", "section"), None, "et"),
        P(("dp", "section"), None),
        P(("dp", "section"), "et", None, None, None),
        P(("dp", "section"), "et", None, None),
    )
    out_specs = P(("dp", "section"), None, "et", None)
    return jax.shard_map(
        per_device, mesh=mesh, in_specs=in_specs, out_specs=out_specs, check_vma=False
    )
```

profile of v0, /device:TPU:6, one launch (start us, length us, event | category | flops | bytes accessed | tf_op | source)
XLA Modules:
  0.0 356.5 jit_solution(17668795315569190571)
XLA Ops:
  6.5 0.0 copy-start
  6.5 0.0 all-gather.3.cloned.1.call-start
  6.5 1.9 collective-permute-start
  8.5 27.3 %collective-permute-done = bf16[1,2,64,4096]{3,2,1,0:T(8,128)(2,1)S(1)} collective-permute-done((bf16[1,2,64,4096]{3,2,1,0:T(8,128)(2,1)}, bf16[1,2,64,4096]{3,2,1,0:T(8,128)(2,1)S(1)}, u32[]{:S(2)}, u32[]{:S(2)}) %collective-permute-start) | collective-permute-done | bytes 1048608 | tf_op jit(solution)/shard_map/ppermute | solution.py:11
  35.8 0.0 copy-start.2
  35.8 0.3 fusion.10
  36.1 0.7 copy-done.2
  36.8 2.0 fusion.8
  38.8 0.0 all-gather.3.cloned.1.call-update
  38.8 0.0 reduce-scatter.2.cloned.1.call-start
  38.8 0.7 convert_element_type.61
  39.5 0.1 copy.16
  39.7 26.8 %all-gather = bf16[1,2,1024,1]{3,1,0,2:T(2,128)(2,1)} all-gather(bf16[1,2,64,1]{3,1,0,2:T(2,128)(2,1)S(1)} %copy.16), channel_id=2, replica_groups=mesh['dp'=2,'section'=8,'et'=16] {'et'}, dimensions={2}, use_global_device_ids=true | all-gather | bytes 4352 | tf_op jit(solution)/shard_map/all_gather | solution.py:39
  66.4 1.4 copy.17
  67.8 0.1 reshape.142
  67.9 0.4 reduce_window_sum.11
  68.4 0.1 broadcast_add_fusion
  68.4 0.1 add_add_fusion
  68.5 0.1 add.87
  68.7 87.8 %all-gather.3.cloned.1.call-done = bf16[2,1024,4096]{2,1,0:T(8,128)(2,1)} async-done(((bf16[2,64,4096]{2,1,0:T(8,128)(2,1)}), bf16[2,1024,4096]{2,1,0:T(8,128)(2,1)}) %all-gather.3.cloned.1.call-update) | async-done | bytes 16777232 | tf_op jit(solution)/shard_map/all_gather | solution.py:38
  156.4 26.9 %scatter_custom_fusion = bf16[769,4096]{1,0:T(8,128)(2,1)} fusion(s32[2048]{0:T(1024)S(1)} %bitcast.42, bf16[2048,4096]{1,0:T(8,128)(2,1)} %bitcast.46, bf16[]{:T(256)} %constant.15.clone.1), kind=kCustom, calls=%fused_computation.6 | custom fusion | bytes 6300160 | tf_op jit(solution)/shard_map/scatter | solution.py:55
  183.3 9.0 %fusion = f32[768,2,384]{2,0,1:T(8,128)S(1)} fusion(bf16[769,4096]{1,0:T(8,128)(2,1)} %scatter_custom_fusion, bf16[4096,2,384]{2,1,0:T(2,128)(2,1)} %bitcast.47), kind=kOutput, calls=%fused_computation.4 | convolution fusion | flops 4831838208 | bytes 14942208 | tf_op jit(solution)/shard_map/rd,dkf->rkf/dot_general | solution.py:21
  192.3 0.0 copy-done
  192.3 3.7 %convolution_convert_fusion = bf16[768,4096]{1,0:T(8,128)(2,1)S(1)} fusion(bf16[1,1,384,4096]{3,2,1,0:T(8,128)(2,1)S(1)} %copy-done, f32[768,2,384]{2,0,1:T(8,128)S(1)} %fusion), kind=kOutput, calls=%fused_computation.2 | convolution fusion | flops 2420834304 | bytes 11796480 | tf_op jit(solution)/shard_map/dot_general | solution.py:23
  196.0 3.1 concatenate.3
  199.1 32.3 %gather_fusion = bf16[2048,4096]{1,0:T(8,128)(2,1)} fusion(bf16[769,4096]{1,0:T(8,128)(2,1)} %concatenate.3, s32[2048]{0:T(1024)S(1)} %broadcast_clamp_fusion), kind=kCustom, calls=%fused_computation | custom fusion | bytes 33562624 | tf_op jit(solution)/shard_map/gather | solution.py:59
  231.3 0.0 copy-start.1
  231.3 0.0 copy-start.3
  231.3 0.0 reduce-scatter.2.cloned.1.call-update
  231.4 115.4 %reduce-scatter.2.cloned.1.call-done = bf16[2,64,4096]{2,1,0:T(8,128)(2,1)} async-done(((bf16[2,1024,4096]{2,1,0:T(8,128)(2,1)}), bf16[2,64,4096]{2,1,0:T(8,128)(2,1)}) %reduce-scatter.2.cloned.1.call-update) | async-done | bytes 1048592 | tf_op jit(solution)/shard_map/reduce_scatter | solution.py:60
  346.7 0.0 copy-done.3
  346.7 2.9 fusion.12
  349.6 0.0 copy-done.1
  (7 shorter events, 0.1 us)
Async XLA Ops:
  6.5 185.8 %copy-start = (bf16[1,1,384,4096]{3,2,1,0:T(8,128)(2,1)S(1)}, bf16[1,1,384,4096]{3,2,1,0:T(8,128)(2,1)}, u32[]{:S(2)}) copy-start(bf16[1,1,384,4096]{3,2,1,0:T(8,128)(2,1)} %param.11) | copy-start | bytes 9437188
  6.5 149.9 %all-gather.3.cloned.1.call-start = ((), (), s32[]{:S(2)}) async-start(), calls=%async_computation.1 | async-start | bytes 17825792 | tf_op jit(solution)/shard_map/all_gather | solution.py:38
  6.5 29.2 %collective-permute-start = (bf16[1,2,64,4096]{3,2,1,0:T(8,128)(2,1)}, bf16[1,2,64,4096]{3,2,1,0:T(8,128)(2,1)S(1)}, u32[]{:S(2)}, u32[]{:S(2)}) collective-permute-start(bf16[1,2,64,4096]{3,2,1,0:T(8,128)(2,1)} %param.6), channel_id=1, source_target_pairs={{0,16},{16,32},{32,48},{48,64},{64,80},{80,96},{96,112},{112,0},{1... | collective-permute-start | bytes 3145736 | tf_op jit(solution)/shard_map/ppermute | solution.py:11
  35.8 1.0 copy-start.2
  38.8 307.9 %reduce-scatter.2.cloned.1.call-start = ((), (), s32[]{:S(2)}) async-start(), calls=%async_computation.2 | async-start | bytes 17825792 | tf_op jit(solution)/shard_map/reduce_scatter | solution.py:60
  231.3 118.3 %copy-start.1 = (bf16[1,1,384,4096]{3,2,1,0:T(8,128)(2,1)S(1)}, bf16[1,1,384,4096]{3,2,1,0:T(8,128)(2,1)}, u32[]{:S(2)}) copy-start(bf16[1,1,384,4096]{3,2,1,0:T(8,128)(2,1)} %param.11) | copy-start | bytes 9437188
  231.3 115.4 %copy-start.3 = (f32[1,2,64]{2,1,0:T(2,128)S(1)}, f32[1,2,64]{2,1,0:T(2,128)}, u32[]{:S(2)}) copy-start(f32[1,2,64]{2,1,0:T(2,128)} %param.8) | copy-start | bytes 1540
Sparse Core Ops, SparseCore 0:
  38.9 117.4 all-gather.2
  231.5 115.1 reduce-scatter.1
where the time goes:
time: 358 us; the launch traced here: 356 us
  waiting for transfers between devices  230 us (64%)
  local copies, waits for them, and re-layouts  64.6 us (18%)
  blocking collectives  26.8 us (7%)
  between operations  13.5 us (4%)
  matrix products  12.6 us (4%)
  other arithmetic  6.56 us (2%)
    reduce_scatter x1, waiting for transfers between devices, per_device(): lax.psum_scatter(terms.astype(jnp.bfloat16), 'et', scatter_dimension=1, t...  115 us
    all_gather x1, waiting for transfers between devices, per_device(): lax.all_gather(normed, 'et', axis=1, tiled=True)  87.8 us
    gather x1, local copies, waits for them, and re-layouts, per_device(): padded[slot_index].astype(jnp.float32)  32.3 us
    ppermute x1, waiting for transfers between devices, passed_along(): lax.ppermute(shard, axis, [(i, (i + by) % size) for i in range(size)])  27.3 us
    scatter x1, local copies, waits for them, and re-layouts, per_device(): buffer = jnp.zeros((slot_total + 1, width), jnp.bfloat16).at[slot_index]....  26.9 us
    all_gather x1, blocking collectives, per_device(): lax.all_gather(chosen.astype(jnp.bfloat16), 'et', axis=1, tiled=True)  26.8 us
    dot_general x1, matrix products, expert_rows(): jnp.einsum('rd,dkf->rkf', buffer, gate_up_w, preferred_element_type=jnp.f...  8.97 us
  transfers between devices with their start and end apart: 3, of which 3 were waited for; matrix products, arithmetic and copies ran while one was open for 1% of the time, Pallas kernels for 0%

commit v1 on v0

v1 whole, which is shorter than its diff:
```python
import jax
import jax.numpy as jnp
from jax import lax
from jax.sharding import PartitionSpec as P

SIDE = 4
F32, BF16 = jnp.float32, jnp.bfloat16


def shift_z(v, by):
    n = lax.axis_size("section")
    return lax.ppermute(v, "section", [(i, (i + by) % n) for i in range(n)])


def shift_x(v, by):
    pairs = [(i, i // SIDE * SIDE + (i + by) % SIDE) for i in range(SIDE * SIDE)]
    return lax.ppermute(v, "et", pairs)


def shift_y(v, by):
    n = SIDE * SIDE
    return lax.ppermute(v, "et", [(i, (i + SIDE * by) % n) for i in range(n)])


def shift_zy(v, by):
    n, m = lax.axis_size("section"), SIDE * SIDE
    pairs = [
        (z * m + i, (z + 1) % n * m + (i + SIDE * by) % m) for z in range(n) for i in range(m)
    ]
    return lax.ppermute(v, ("section", "et"), pairs)


def gather_x(block):
    half = block.shape[0] // 2
    left, right = shift_x(block, 1), shift_x(block, -1)
    far = [shift_x(left[:half], 1), shift_x(right[half:], -1)]
    return jnp.concatenate([block, left, *far, right], 0)


def scatter_sum_x(parts):
    half = parts[0].shape[0] // 2
    add = lambda a, b: (a.astype(F32) + b.astype(F32)).astype(BF16)
    to_right = shift_x(parts[2][:half], 1)
    to_left = shift_x(parts[2][half:], -1)
    right = jnp.concatenate([add(parts[3][:half], to_right), parts[3][half:]], 0)
    left = jnp.concatenate([parts[1][:half], add(parts[1][half:], to_left)], 0)
    from_left, from_right = shift_x(right, 1), shift_x(left, -1)
    return parts[0].astype(F32) + from_left.astype(F32) + from_right.astype(F32)


def slot_map(ids, row, cap):
    toks = ids.shape[0]
    same = (ids[:, None] == ids[None, :]) & (
        jnp.arange(toks)[:, None] > jnp.arange(toks)[None, :]
    )
    rank = jnp.sum(same.astype(jnp.int32), axis=1)
    target = (ids - row) % SIDE * cap + rank
    slots = jnp.arange(SIDE * cap)[:, None] == target[None, :]
    return slots.astype(BF16).reshape(SIDE, cap, toks)


def normalize(rows, gain):
    values = rows.astype(F32)
    scale = lax.rsqrt(jnp.mean(values * values, axis=-1, keepdims=True) + 1e-06)
    return (values * scale * gain).astype(BF16)


def per_device(acts, expert_ids, gates, norm_gain, w_gate_up, w_down):
    _, batches, toks, width = acts.shape
    cap = min(toks, 3 * toks // (2 * SIDE))
    row = lax.axis_index("et") // SIDE
    ids = expert_ids[0, :, :, 0]
    asked = shift_z(jnp.concatenate([ids.reshape(-1).astype(F32), norm_gain[0]]), -1)
    next_ids = asked[: batches * toks].astype(jnp.int32).reshape(batches, toks)
    next_gain = asked[batches * toks :]

    mine = []
    for b in range(batches):
        normed = normalize(acts[0, b], next_gain)
        to_slots = slot_map(next_ids[b], row, cap)
        mine.append(
            jnp.concatenate(
                [
                    shift_zy(
                        jnp.dot(to_slots[k], normed, preferred_element_type=F32).astype(BF16), k
                    )
                    for k in range(SIDE)
                ],
                0,
            )
        )

    hidden = []
    for b in range(batches):
        rows = gather_x(mine[b])
        both = jnp.einsum("rd,dkf->rkf", rows, w_gate_up[0, 0], preferred_element_type=F32)
        hidden.append((jax.nn.silu(both[:, 0]) * both[:, 1]).astype(BF16))

    held = acts[0] * (1.0 + 0.0 * mine[-1][0, 0])
    arriving = shift_z(held, 1)
    outs = []
    for b in range(batches):
        part = jnp.dot(hidden[b], w_down[0, 0], preferred_element_type=F32).astype(BF16)
        part = part.reshape(SIDE, SIDE * cap, width)
        summed = scatter_sum_x([part[j] for j in range(SIDE)]).astype(BF16)
        summed = summed.reshape(SIDE, cap, width)
        back = [summed[0]] + [shift_y(summed[k], -k) for k in range(1, SIDE)]
        from_slots = slot_map(ids[b], row, cap).reshape(SIDE * cap, toks).T
        sums = jnp.dot(from_slots, jnp.concatenate(back, 0), preferred_element_type=F32)
        outs.append((arriving[b].astype(F32) + gates[0, b][:, None] * sums).astype(BF16))
    return jnp.stack(outs)[None]


def solution(mesh):
    in_specs = (
        P(("dp", "section"), None, "et", None),
        P(("dp", "section"), None, "et", None),
        P(("dp", "section"), None, "et"),
        P(("dp", "section"), None),
        P(("dp", "section"), "et", None, None, None),
        P(("dp", "section"), "et", None, None),
    )
    out_specs = P(("dp", "section"), None, "et", None)
    return jax.shard_map(
        per_device, mesh=mesh, in_specs=in_specs, out_specs=out_specs, check_vma=False
    )
```

time: 358 us -> 161 us (0.45)
  waiting for transfers between devices: 230 us -> 92.7 us
  local copies, waits for them, and re-layouts: 64.6 us -> 3.07 us
  starting transfers between devices: 1.96 us -> 42.1 us
  blocking collectives: 26.8 us -> 0 us
  between operations: 13.5 us -> 1.19 us
    reduce_scatter x1 -> x0, waiting for transfers between devices: 115 us -> none  [per_device(): lax.psum_scatter(terms.astype(jnp.bfloat16), 'et', scatter_dimension=1, t...]
    all_gather x1 -> x0, waiting for transfers between devices: 87.8 us -> none  [per_device(): lax.all_gather(normed, 'et', axis=1, tiled=True)]
    ppermute x1 -> x32, waiting for transfers between devices: 27.3 us -> 92.7 us  [the longest x16 58.6 us: shift_x(): return lax.ppermute(v, 'et', pairs)]
    ppermute x1 -> x32, starting transfers between devices: 1.92 us -> 42.1 us  [the longest x16 15.7 us: shift_x(): return lax.ppermute(v, 'et', pairs)]
    gather x1 -> x0, local copies, waits for them, and re-layouts: 32.3 us -> none  [per_device(): padded[slot_index].astype(jnp.float32)]
    scatter x1 -> x0, local copies, waits for them, and re-layouts: 26.9 us -> none  [per_device(): buffer = jnp.zeros((slot_total + 1, width), jnp.bfloat16).at[slot_index]....]
    all_gather x1 -> x0, blocking collectives: 26.8 us -> none  [per_device(): lax.all_gather(chosen.astype(jnp.bfloat16), 'et', axis=1, tiled=True)]
    dot_general x2 -> x14, matrix products: 12.6 us -> 15.1 us  [the longest x8 5.57 us: per_device(): jnp.dot(to_slots[k], normed, preferred_element_type=F32).astype(BF16)]
  transfers between devices with their start and end apart: 3 -> 32, of which waited for: 3 -> 24; matrix products, arithmetic and copies ran while one was open for 1% -> 10% of each run, Pallas kernels for 0% -> 0%
where the time goes in v1:
time: 161 us
  waiting for transfers between devices  92.7 us (58%)
  starting transfers between devices  42.1 us (26%)
  matrix products  15.1 us (9%)
  other arithmetic  6.94 us (4%)
  local copies, waits for them, and re-layouts  3.07 us (2%)
    ppermute x16, waiting for transfers between devices, shift_x(): return lax.ppermute(v, 'et', pairs)  58.6 us
    ppermute x8, waiting for transfers between devices, shift_zy(): return lax.ppermute(v, ('section', 'et'), pairs)  25.8 us
    ppermute x16, starting transfers between devices, shift_x(): return lax.ppermute(v, 'et', pairs)  15.7 us
    ppermute x8, starting transfers between devices, shift_zy(): return lax.ppermute(v, ('section', 'et'), pairs)  10.5 us
    ppermute x6, starting transfers between devices, shift_y(): return lax.ppermute(v, 'et', [(i, (i + SIDE * by) % n) for i in range(n)])  9.96 us
    ppermute x6, waiting for transfers between devices, shift_y(): return lax.ppermute(v, 'et', [(i, (i + SIDE * by) % n) for i in range(n)])  8.38 us
    ppermute x2, starting transfers between devices, shift_z(): return lax.ppermute(v, 'section', [(i, (i + by) % n) for i in range(n)])  5.94 us
    dot_general x8, matrix products, per_device(): jnp.dot(to_slots[k], normed, preferred_element_type=F32).astype(BF16)  5.57 us
  transfers between devices with their start and end apart: 32, of which 24 were waited for; matrix products, arithmetic and copies ran while one was open for 10% of the time, Pallas kernels for 0%

profile of v1, /device:TPU:6, one launch (start us, length us, event | category | flops | bytes accessed | tf_op | source)
XLA Modules:
  0.0 161.1 jit_solution(15330185201542688106)
XLA Ops:
  0.0 0.8 convert_reduce_fusion.4
  1.7 5.9 %collective-permute-start = (f32[4224]{0:T(1024)S(1)}, f32[4224]{0:T(1024)S(1)}, u32[]{:S(2)}, u32[]{:S(2)}) collective-permute-start(f32[4224]{0:T(1024)S(1)} %pad_maximum_fusion.4), channel_id=1, source_target_pairs={{0,112},{16,0},{32,16},{48,32},{64,48},{80,64},{96,80},{112,96},{1... | collective-permute-start | bytes 50696 | tf_op jit(solution)/shard_map/ppermute | solution.py:12
  8.2 1.5 fusion.11
  11.8 1.4 convolution_convert_fusion.8
  13.2 1.4 convolution_convert_fusion.7
  14.5 1.4 convolution_convert_fusion.6
  17.6 4.2 %collective-permute-start.5 = (bf16[24,4096]{1,0:T(8,128)(2,1)S(1)}, bf16[24,4096]{1,0:T(8,128)(2,1)S(1)}, u32[]{:S(2)}, u32[]{:S(2)}) collective-permute-start(bf16[24,4096]{1,0:T(8,128)(2,1)S(1)} %convolution_convert_fusion.6), channel_id=1, source_target_pairs={{0,24},{1,25},{2,26},{3,27},{4,28},{5,29},{6,30},{7,31},{8,16},{9,... | collective-permute-start | bytes 589832 | tf_op jit(solution)/shard_map/ppermute | solution.py:30
  21.8 3.0 %collective-permute-start.6 = (bf16[24,4096]{1,0:T(8,128)(2,1)S(1)}, bf16[24,4096]{1,0:T(8,128)(2,1)S(1)}, u32[]{:S(2)}, u32[]{:S(2)}) collective-permute-start(bf16[24,4096]{1,0:T(8,128)(2,1)S(1)} %convolution_convert_fusion.5), channel_id=1, source_target_pairs={{0,28},{1,29},{2,30},{3,31},{4,16},{5,17},{6,18},{7,19},{8,20},{9,... | collective-permute-start | bytes 589832 | tf_op jit(solution)/shard_map/ppermute | solution.py:30
  24.8 1.9 %collective-permute-start.1 = (bf16[24,4096]{1,0:T(8,128)(2,1)S(1)}, bf16[24,4096]{1,0:T(8,128)(2,1)S(1)}, u32[]{:S(2)}, u32[]{:S(2)}) collective-permute-start(bf16[24,4096]{1,0:T(8,128)(2,1)S(1)} %convolution_convert_fusion.9), channel_id=1, source_target_pairs={{0,16},{1,17},{2,18},{3,19},{4,20},{5,21},{6,22},{7,23},{8,24},{9,... | collective-permute-start | bytes 589832 | tf_op jit(solution)/shard_map/ppermute | solution.py:30
  27.0 1.2 collective-permute-start.18
  28.2 5.0 %collective-permute-done.4 = bf16[24,4096]{1,0:T(8,128)(2,1)S(1)} collective-permute-done((bf16[24,4096]{1,0:T(8,128)(2,1)S(1)}, bf16[24,4096]{1,0:T(8,128)(2,1)S(1)}, u32[]{:S(2)}, u32[]{:S(2)}) %collective-permute-start.4) | collective-permute-done | bytes 196640 | tf_op jit(solution)/shard_map/ppermute | solution.py:30
  33.2 4.4 %collective-permute-done.5 = bf16[24,4096]{1,0:T(8,128)(2,1)S(1)} collective-permute-done((bf16[24,4096]{1,0:T(8,128)(2,1)S(1)}, bf16[24,4096]{1,0:T(8,128)(2,1)S(1)}, u32[]{:S(2)}, u32[]{:S(2)}) %collective-permute-start.5) | collective-permute-done | bytes 196640 | tf_op jit(solution)/shard_map/ppermute | solution.py:30
  37.6 2.6 %collective-permute-done.6 = bf16[24,4096]{1,0:T(8,128)(2,1)S(1)} collective-permute-done((bf16[24,4096]{1,0:T(8,128)(2,1)S(1)}, bf16[24,4096]{1,0:T(8,128)(2,1)S(1)}, u32[]{:S(2)}, u32[]{:S(2)}) %collective-permute-start.6) | collective-permute-done | bytes 196640 | tf_op jit(solution)/shard_map/ppermute | solution.py:30
  40.8 2.6 %collective-permute-done.1 = bf16[24,4096]{1,0:T(8,128)(2,1)S(1)} collective-permute-done((bf16[24,4096]{1,0:T(8,128)(2,1)S(1)}, bf16[24,4096]{1,0:T(8,128)(2,1)S(1)}, u32[]{:S(2)}, u32[]{:S(2)}) %collective-permute-start.1) | collective-permute-done | bytes 196640 | tf_op jit(solution)/shard_map/ppermute | solution.py:30
  44.2 5.8 %collective-permute-done.18 = bf16[24,4096]{1,0:T(8,128)(2,1)S(1)} collective-permute-done((bf16[24,4096]{1,0:T(8,128)(2,1)S(1)}, bf16[24,4096]{1,0:T(8,128)(2,1)S(1)}, u32[]{:S(2)}, u32[]{:S(2)}) %collective-permute-start.18) | collective-permute-done | bytes 196640 | tf_op jit(solution)/shard_map/ppermute | solution.py:30
  50.1 4.4 %collective-permute-done.19 = bf16[24,4096]{1,0:T(8,128)(2,1)S(1)} collective-permute-done((bf16[24,4096]{1,0:T(8,128)(2,1)S(1)}, bf16[24,4096]{1,0:T(8,128)(2,1)S(1)}, u32[]{:S(2)}, u32[]{:S(2)}) %collective-permute-start.19) | collective-permute-done | bytes 196640 | tf_op jit(solution)/shard_map/ppermute | solution.py:30
  54.5 1.1 collective-permute-done.20
  56.2 1.5 collective-permute-start.23
  59.1 1.8 %collective-permute-start.8 = (bf16[48,4096]{1,0:T(8,128)(2,1)S(1)}, bf16[48,4096]{1,0:T(8,128)(2,1)S(1)}, u32[]{:S(2)}, u32[]{:S(2)}) collective-permute-start(bf16[48,4096]{1,0:T(8,128)(2,1)S(1)} %slice.265), channel_id=1, source_target_pairs={{0,1},{1,2},{2,3},{3,0},{4,5},{5,6},{6,7},{7,4},{8,9},{9,10},{10,1... | collective-permute-start | bytes 1179656 | tf_op jit(solution)/shard_map/ppermute | solution.py:17
  60.9 3.1 %collective-permute-done.9 = bf16[96,4096]{1,0:T(8,128)(2,1)S(1)} collective-permute-done((bf16[96,4096]{1,0:T(8,128)(2,1)S(1)}, bf16[96,4096]{1,0:T(8,128)(2,1)S(1)}, u32[]{:S(2)}, u32[]{:S(2)}) %collective-permute-start.9) | collective-permute-done | bytes 786464 | tf_op jit(solution)/shard_map/ppermute | solution.py:17
  64.1 12.0 %collective-permute-done.21 = bf16[96,4096]{1,0:T(8,128)(2,1)S(1)} collective-permute-done((bf16[96,4096]{1,0:T(8,128)(2,1)S(1)}, bf16[96,4096]{1,0:T(8,128)(2,1)S(1)}, u32[]{:S(2)}, u32[]{:S(2)}) %collective-permute-start.21) | collective-permute-done | bytes 786464 | tf_op jit(solution)/shard_map/ppermute | solution.py:17
  76.2 1.8 %collective-permute-start.22 = (bf16[48,4096]{1,0:T(8,128)(2,1)S(1)}, bf16[48,4096]{1,0:T(8,128)(2,1)S(1)}, u32[]{:S(2)}, u32[]{:S(2)}) collective-permute-start(bf16[48,4096]{1,0:T(8,128)(2,1)S(1)} %slice.284), channel_id=1, source_target_pairs={{0,1},{1,2},{2,3},{3,0},{4,5},{5,6},{6,7},{7,4},{8,9},{9,10},{10,1... | collective-permute-start | bytes 1179656 | tf_op jit(solution)/shard_map/ppermute | solution.py:17
  78.0 2.9 %collective-permute-done.23 = bf16[96,4096]{1,0:T(8,128)(2,1)S(1)} collective-permute-done((bf16[96,4096]{1,0:T(8,128)(2,1)S(1)}, bf16[96,4096]{1,0:T(8,128)(2,1)S(1)}, u32[]{:S(2)}, u32[]{:S(2)}) %collective-permute-start.23) | collective-permute-done | bytes 786464 | tf_op jit(solution)/shard_map/ppermute | solution.py:17
  81.1 3.5 %collective-permute-done.8 = bf16[48,4096]{1,0:T(8,128)(2,1)S(1)} collective-permute-done((bf16[48,4096]{1,0:T(8,128)(2,1)S(1)}, bf16[48,4096]{1,0:T(8,128)(2,1)S(1)}, u32[]{:S(2)}, u32[]{:S(2)}) %collective-permute-start.8) | collective-permute-done | bytes 393248 | tf_op jit(solution)/shard_map/ppermute | solution.py:17
  84.6 4.6 %collective-permute-done.10 = bf16[48,4096]{1,0:T(8,128)(2,1)S(1)} collective-permute-done((bf16[48,4096]{1,0:T(8,128)(2,1)S(1)}, bf16[48,4096]{1,0:T(8,128)(2,1)S(1)}, u32[]{:S(2)}, u32[]{:S(2)}) %collective-permute-start.10) | collective-permute-done | bytes 393248 | tf_op jit(solution)/shard_map/ppermute | solution.py:17
  89.4 2.6 %fusion.2 = f32[384,2,384]{2,0,1:T(8,128)S(1)} fusion(bf16[4096,2,384]{2,1,0:T(2,128)(2,1)S(1)} %bitcast.67, bf16[384,4096]{1,0:T(8,128)(2,1)S(1)} %constant_dynamic-update-slice_fusion.4), kind=kOutput, calls=%fused_computation.4 | convolution fusion | flops 2415919104 | bytes 10616832 | tf_op jit(solution)/shard_map/rd,dkf->rkf/dot_general | solution.py:96
  92.0 1.8 %convolution_convert_fusion.1 = bf16[384,4096]{1,0:T(8,128)(2,1)S(1)} fusion(bf16[1,1,384,4096]{3,2,1,0:T(8,128)(2,1)S(1)} %copy-done, f32[384,2,384]{2,0,1:T(8,128)S(1)} %fusion.2), kind=kOutput, calls=%fused_computation.1 | convolution fusion | flops 1210417152 | bytes 7471104 | tf_op jit(solution)/shard_map/dot_general | solution.py:103
  94.1 2.0 %collective-permute-start.13 = (bf16[48,4096]{1,0:T(8,128)(2,1)S(1)}, bf16[48,4096]{1,0:T(8,128)(2,1)S(1)}, u32[]{:S(2)}, u32[]{:S(2)}) collective-permute-start(bf16[48,4096]{1,0:T(8,128)(2,1)S(1)} %get-tuple-element.10), channel_id=1, source_target_pairs={{0,3},{1,0},{2,1},{3,2},{4,7},{5,4},{6,5},{7,6},{8,11},{9,8},{10,9... | collective-permute-start | bytes 1179656 | tf_op jit(solution)/shard_map/ppermute | solution.py:17
  96.1 0.9 collective-permute-done.24
  97.1 2.6 %fusion = f32[384,2,384]{2,0,1:T(8,128)S(1)} fusion(bf16[4096,2,384]{2,1,0:T(2,128)(2,1)S(1)} %bitcast.68, bf16[384,4096]{1,0:T(8,128)(2,1)S(1)} %constant_dynamic-update-slice_fusion.16), kind=kOutput, calls=%fused_computation.2 | convolution fusion | flops 2415919104 | bytes 10616832 | tf_op jit(solution)/shard_map/rd,dkf->rkf/dot_general | solution.py:96
  99.7 1.8 %convolution_convert_fusion = bf16[384,4096]{1,0:T(8,128)(2,1)S(1)} fusion(bf16[1,1,384,4096]{3,2,1,0:T(8,128)(2,1)S(1)} %copy-done, f32[384,2,384]{2,0,1:T(8,128)S(1)} %fusion), kind=kOutput, calls=%fused_computation | convolution fusion | flops 1210417152 | bytes 7471104 | tf_op jit(solution)/shard_map/dot_general | solution.py:103
  102.4 1.4 collective-permute-start.27
  104.0 1.8 %collective-permute-done.13 = bf16[48,4096]{1,0:T(8,128)(2,1)S(1)} collective-permute-done((bf16[48,4096]{1,0:T(8,128)(2,1)S(1)}, bf16[48,4096]{1,0:T(8,128)(2,1)S(1)}, u32[]{:S(2)}, u32[]{:S(2)}) %collective-permute-start.13) | collective-permute-done | bytes 393248 | tf_op jit(solution)/shard_map/ppermute | solution.py:17
  106.1 2.1 %collective-permute-start.14 = (bf16[96,4096]{1,0:T(8,128)(2,1)S(1)}, bf16[96,4096]{1,0:T(8,128)(2,1)S(1)}, u32[]{:S(2)}, u32[]{:S(2)}) collective-permute-start(bf16[96,4096]{1,0:T(8,128)(2,1)S(1)} %pad_maximum_fusion.1), channel_id=1, source_target_pairs={{0,3},{1,0},{2,1},{3,2},{4,7},{5,4},{6,5},{7,6},{8,11},{9,8},{10,9... | collective-permute-start | bytes 2359304 | tf_op jit(solution)/shard_map/ppermute | solution.py:17
  108.2 5.6 %collective-permute-done.25 = bf16[48,4096]{1,0:T(8,128)(2,1)S(1)} collective-permute-done((bf16[48,4096]{1,0:T(8,128)(2,1)S(1)}, bf16[48,4096]{1,0:T(8,128)(2,1)S(1)}, u32[]{:S(2)}, u32[]{:S(2)}) %collective-permute-start.25) | collective-permute-done | bytes 393248 | tf_op jit(solution)/shard_map/ppermute | solution.py:17
  113.8 1.8 %collective-permute-done.27 = bf16[48,4096]{1,0:T(8,128)(2,1)S(1)} collective-permute-done((bf16[48,4096]{1,0:T(8,128)(2,1)S(1)}, bf16[48,4096]{1,0:T(8,128)(2,1)S(1)}, u32[]{:S(2)}, u32[]{:S(2)}) %collective-permute-start.27) | collective-permute-done | bytes 393248 | tf_op jit(solution)/shard_map/ppermute | solution.py:17
  116.0 2.1 %collective-permute-start.28 = (bf16[96,4096]{1,0:T(8,128)(2,1)S(1)}, bf16[96,4096]{1,0:T(8,128)(2,1)S(1)}, u32[]{:S(2)}, u32[]{:S(2)}) collective-permute-start(bf16[96,4096]{1,0:T(8,128)(2,1)S(1)} %pad_maximum_fusion.3), channel_id=1, source_target_pairs={{0,3},{1,0},{2,1},{3,2},{4,7},{5,4},{6,5},{7,6},{8,11},{9,8},{10,9... | collective-permute-start | bytes 2359304 | tf_op jit(solution)/shard_map/ppermute | solution.py:17
  118.1 12.5 %collective-permute-done.12 = bf16[96,4096]{1,0:T(8,128)(2,1)S(1)} collective-permute-done((bf16[96,4096]{1,0:T(8,128)(2,1)S(1)}, bf16[96,4096]{1,0:T(8,128)(2,1)S(1)}, u32[]{:S(2)}, u32[]{:S(2)}) %collective-permute-start.12) | collective-permute-done | bytes 786464 | tf_op jit(solution)/shard_map/ppermute | solution.py:17
  130.6 1.8 %collective-permute-done.14 = bf16[96,4096]{1,0:T(8,128)(2,1)S(1)} collective-permute-done((bf16[96,4096]{1,0:T(8,128)(2,1)S(1)}, bf16[96,4096]{1,0:T(8,128)(2,1)S(1)}, u32[]{:S(2)}, u32[]{:S(2)}) %collective-permute-start.14) | collective-permute-done | bytes 786464 | tf_op jit(solution)/shard_map/ppermute | solution.py:17
  132.8 3.7 %collective-permute-start.15 = (bf16[24,4096]{1,0:T(8,128)(2,1)S(1)}, bf16[24,4096]{1,0:T(8,128)(2,1)S(1)}, u32[]{:S(2)}, u32[]{:S(2)}) collective-permute-start(bf16[24,4096]{1,0:T(8,128)(2,1)S(1)} %get-tuple-element.22), channel_id=1, source_target_pairs={{0,12},{1,13},{2,14},{3,15},{4,0},{5,1},{6,2},{7,3},{8,4},{9,5},{1... | collective-permute-start | bytes 589832 | tf_op jit(solution)/shard_map/ppermute | solution.py:22
  136.5 7.4 %collective-permute-done.26 = bf16[96,4096]{1,0:T(8,128)(2,1)S(1)} collective-permute-done((bf16[96,4096]{1,0:T(8,128)(2,1)S(1)}, bf16[96,4096]{1,0:T(8,128)(2,1)S(1)}, u32[]{:S(2)}, u32[]{:S(2)}) %collective-permute-start.26) | collective-permute-done | bytes 786464 | tf_op jit(solution)/shard_map/ppermute | solution.py:17
  144.0 1.2 collective-permute-start.17
  145.8 3.7 %collective-permute-start.29 = (bf16[24,4096]{1,0:T(8,128)(2,1)S(1)}, bf16[24,4096]{1,0:T(8,128)(2,1)S(1)}, u32[]{:S(2)}, u32[]{:S(2)}) collective-permute-start(bf16[24,4096]{1,0:T(8,128)(2,1)S(1)} %get-tuple-element.26), channel_id=1, source_target_pairs={{0,12},{1,13},{2,14},{3,15},{4,0},{5,1},{6,2},{7,3},{8,4},{9,5},{1... | collective-permute-start | bytes 589832 | tf_op jit(solution)/shard_map/ppermute | solution.py:22
  149.9 1.0 collective-permute-start.31
  150.9 4.6 %collective-permute-done.17 = bf16[24,4096]{1,0:T(8,128)(2,1)S(1)} collective-permute-done((bf16[24,4096]{1,0:T(8,128)(2,1)S(1)}, bf16[24,4096]{1,0:T(8,128)(2,1)S(1)}, u32[]{:S(2)}, u32[]{:S(2)}) %collective-permute-start.17) | collective-permute-done | bytes 196640 | tf_op jit(solution)/shard_map/ppermute | solution.py:22
  155.9 2.3 %collective-permute-done.30 = bf16[24,4096]{1,0:T(8,128)(2,1)S(1)} collective-permute-done((bf16[24,4096]{1,0:T(8,128)(2,1)S(1)}, bf16[24,4096]{1,0:T(8,128)(2,1)S(1)}, u32[]{:S(2)}, u32[]{:S(2)}) %collective-permute-start.30) | collective-permute-done | bytes 196640 | tf_op jit(solution)/shard_map/ppermute | solution.py:22
  158.2 1.5 collective-permute-done.31
  160.0 1.1 maximum_bitcast_fusion
  (92 shorter events, 13.1 us)
Async XLA Ops:
  0.0 92.0 %copy-start = (bf16[1,1,384,4096]{3,2,1,0:T(8,128)(2,1)S(1)}, bf16[1,1,384,4096]{3,2,1,0:T(8,128)(2,1)}, u32[]{:S(2)}) copy-start(bf16[1,1,384,4096]{3,2,1,0:T(8,128)(2,1)} %param.11) | copy-start | bytes 9437188
  1.7 9.8 %collective-permute-start = (f32[4224]{0:T(1024)S(1)}, f32[4224]{0:T(1024)S(1)}, u32[]{:S(2)}, u32[]{:S(2)}) collective-permute-start(f32[4224]{0:T(1024)S(1)} %pad_maximum_fusion.4), channel_id=1, source_target_pairs={{0,112},{16,0},{32,16},{48,32},{64,48},{80,64},{96,80},{112,96},{1... | collective-permute-start | bytes 50696 | tf_op jit(solution)/shard_map/ppermute | solution.py:12
  10.5 5.4 %copy-start.1 = (bf16[1,2,64,4096]{3,2,1,0:T(8,128)(2,1)S(1)}, bf16[1,2,64,4096]{3,2,1,0:T(8,128)(2,1)}, u32[]{:S(2)}) copy-start(bf16[1,2,64,4096]{3,2,1,0:T(8,128)(2,1)} %param.6) | copy-start | bytes 3145732
  17.4 9.6 %collective-permute-start.3 = (bf16[24,4096]{1,0:T(8,128)(2,1)S(1)}, bf16[24,4096]{1,0:T(8,128)(2,1)S(1)}, u32[]{:S(2)}, u32[]{:S(2)}) collective-permute-start(bf16[24,4096]{1,0:T(8,128)(2,1)S(1)} %convolution_convert_fusion.8), channel_id=1, source_target_pairs={{0,16},{1,17},{2,18},{3,19},{4,20},{5,21},{6,22},{7,23},{8,24},{9,... | collective-permute-start | bytes 589832 | tf_op jit(solution)/shard_map/ppermute | solution.py:30
  17.5 15.7 %collective-permute-start.4 = (bf16[24,4096]{1,0:T(8,128)(2,1)S(1)}, bf16[24,4096]{1,0:T(8,128)(2,1)S(1)}, u32[]{:S(2)}, u32[]{:S(2)}) collective-permute-start(bf16[24,4096]{1,0:T(8,128)(2,1)S(1)} %convolution_convert_fusion.7), channel_id=1, source_target_pairs={{0,20},{1,21},{2,22},{3,23},{4,24},{5,25},{6,26},{7,27},{8,28},{9,... | collective-permute-start | bytes 589832 | tf_op jit(solution)/shard_map/ppermute | solution.py:30
  17.6 20.0 %collective-permute-start.5 = (bf16[24,4096]{1,0:T(8,128)(2,1)S(1)}, bf16[24,4096]{1,0:T(8,128)(2,1)S(1)}, u32[]{:S(2)}, u32[]{:S(2)}) collective-permute-start(bf16[24,4096]{1,0:T(8,128)(2,1)S(1)} %convolution_convert_fusion.6), channel_id=1, source_target_pairs={{0,24},{1,25},{2,26},{3,27},{4,28},{5,29},{6,30},{7,31},{8,16},{9,... | collective-permute-start | bytes 589832 | tf_op jit(solution)/shard_map/ppermute | solution.py:30
  21.8 18.4 %collective-permute-start.6 = (bf16[24,4096]{1,0:T(8,128)(2,1)S(1)}, bf16[24,4096]{1,0:T(8,128)(2,1)S(1)}, u32[]{:S(2)}, u32[]{:S(2)}) collective-permute-start(bf16[24,4096]{1,0:T(8,128)(2,1)S(1)} %convolution_convert_fusion.5), channel_id=1, source_target_pairs={{0,28},{1,29},{2,30},{3,31},{4,16},{5,17},{6,18},{7,19},{8,20},{9,... | collective-permute-start | bytes 589832 | tf_op jit(solution)/shard_map/ppermute | solution.py:30
  24.8 18.6 %collective-permute-start.1 = (bf16[24,4096]{1,0:T(8,128)(2,1)S(1)}, bf16[24,4096]{1,0:T(8,128)(2,1)S(1)}, u32[]{:S(2)}, u32[]{:S(2)}) collective-permute-start(bf16[24,4096]{1,0:T(8,128)(2,1)S(1)} %convolution_convert_fusion.9), channel_id=1, source_target_pairs={{0,16},{1,17},{2,18},{3,19},{4,20},{5,21},{6,22},{7,23},{8,24},{9,... | collective-permute-start | bytes 589832 | tf_op jit(solution)/shard_map/ppermute | solution.py:30
  27.0 23.1 %collective-permute-start.18 = (bf16[24,4096]{1,0:T(8,128)(2,1)S(1)}, bf16[24,4096]{1,0:T(8,128)(2,1)S(1)}, u32[]{:S(2)}, u32[]{:S(2)}) collective-permute-start(bf16[24,4096]{1,0:T(8,128)(2,1)S(1)} %convolution_convert_fusion.4), channel_id=1, source_target_pairs={{0,20},{1,21},{2,22},{3,23},{4,24},{5,25},{6,26},{7,27},{8,28},{9,... | collective-permute-start | bytes 589832 | tf_op jit(solution)/shard_map/ppermute | solution.py:30
  33.2 21.2 %collective-permute-start.19 = (bf16[24,4096]{1,0:T(8,128)(2,1)S(1)}, bf16[24,4096]{1,0:T(8,128)(2,1)S(1)}, u32[]{:S(2)}, u32[]{:S(2)}) collective-permute-start(bf16[24,4096]{1,0:T(8,128)(2,1)S(1)} %convolution_convert_fusion.3), channel_id=1, source_target_pairs={{0,24},{1,25},{2,26},{3,27},{4,28},{5,29},{6,30},{7,31},{8,16},{9,... | collective-permute-start | bytes 589832 | tf_op jit(solution)/shard_map/ppermute | solution.py:30
  37.6 18.0 %collective-permute-start.20 = (bf16[24,4096]{1,0:T(8,128)(2,1)S(1)}, bf16[24,4096]{1,0:T(8,128)(2,1)S(1)}, u32[]{:S(2)}, u32[]{:S(2)}) collective-permute-start(bf16[24,4096]{1,0:T(8,128)(2,1)S(1)} %convolution_convert_fusion.2), channel_id=1, source_target_pairs={{0,28},{1,29},{2,30},{3,31},{4,16},{5,17},{6,18},{7,19},{8,20},{9,... | collective-permute-start | bytes 589832 | tf_op jit(solution)/shard_map/ppermute | solution.py:30
  40.2 49.2 %slice-start = ((s8[6291456]{0:T(1024)(128)(4,1)}), s8[4194304]{0:T(1024)(128)(4,1)S(1)}, s32[]{:S(2)}) async-start(s8[6291456]{0:T(1024)(128)(4,1)} %bitcast.65), calls=%async_computation | async-start | bytes 8388608
  40.2 18.8 %collective-permute-start.7 = (bf16[96,4096]{1,0:T(8,128)(2,1)S(1)}, bf16[96,4096]{1,0:T(8,128)(2,1)S(1)}, u32[]{:S(2)}, u32[]{:S(2)}) collective-permute-start(bf16[96,4096]{1,0:T(8,128)(2,1)S(1)} %get-tuple-element.27), channel_id=1, source_target_pairs={{0,1},{1,2},{2,3},{3,0},{4,5},{5,6},{6,7},{7,4},{8,9},{9,10},{10,1... | collective-permute-start | bytes 2359304 | tf_op jit(solution)/shard_map/ppermute | solution.py:17
  43.4 20.6 %collective-permute-start.9 = (bf16[96,4096]{1,0:T(8,128)(2,1)S(1)}, bf16[96,4096]{1,0:T(8,128)(2,1)S(1)}, u32[]{:S(2)}, u32[]{:S(2)}) collective-permute-start(bf16[96,4096]{1,0:T(8,128)(2,1)S(1)} %get-tuple-element.27), channel_id=1, source_target_pairs={{0,3},{1,0},{2,1},{3,2},{4,7},{5,4},{6,5},{7,6},{8,11},{9,8},{10,9... | collective-permute-start | bytes 2359304 | tf_op jit(solution)/shard_map/ppermute | solution.py:17
  55.6 20.6 %collective-permute-start.21 = (bf16[96,4096]{1,0:T(8,128)(2,1)S(1)}, bf16[96,4096]{1,0:T(8,128)(2,1)S(1)}, u32[]{:S(2)}, u32[]{:S(2)}) collective-permute-start(bf16[96,4096]{1,0:T(8,128)(2,1)S(1)} %get-tuple-element.35), channel_id=1, source_target_pairs={{0,1},{1,2},{2,3},{3,0},{4,5},{5,6},{6,7},{7,4},{8,9},{9,10},{10,1... | collective-permute-start | bytes 2359304 | tf_op jit(solution)/shard_map/ppermute | solution.py:17
  56.2 24.7 %collective-permute-start.23 = (bf16[96,4096]{1,0:T(8,128)(2,1)S(1)}, bf16[96,4096]{1,0:T(8,128)(2,1)S(1)}, u32[]{:S(2)}, u32[]{:S(2)}) collective-permute-start(bf16[96,4096]{1,0:T(8,128)(2,1)S(1)} %get-tuple-element.35), channel_id=1, source_target_pairs={{0,3},{1,0},{2,1},{3,2},{4,7},{5,4},{6,5},{7,6},{8,11},{9,8},{10,9... | collective-permute-start | bytes 2359304 | tf_op jit(solution)/shard_map/ppermute | solution.py:17
  59.0 90.6 %collective-permute-start.2 = (bf16[2,64,4096]{2,1,0:T(8,128)(2,1)S(1)}, bf16[2,64,4096]{2,1,0:T(8,128)(2,1)S(1)}, u32[]{:S(2)}, u32[]{:S(2)}) collective-permute-start(bf16[2,64,4096]{2,1,0:T(8,128)(2,1)S(1)} %multiply_bitcast_fusion), channel_id=1, source_target_pairs={{0,16},{16,32},{32,48},{48,64},{64,80},{80,96},{96,112},{112,0},{1... | collective-permute-start | bytes 3145736 | tf_op jit(solution)/shard_map/ppermute | solution.py:12
  59.1 25.5 %collective-permute-start.8 = (bf16[48,4096]{1,0:T(8,128)(2,1)S(1)}, bf16[48,4096]{1,0:T(8,128)(2,1)S(1)}, u32[]{:S(2)}, u32[]{:S(2)}) collective-permute-start(bf16[48,4096]{1,0:T(8,128)(2,1)S(1)} %slice.265), channel_id=1, source_target_pairs={{0,1},{1,2},{2,3},{3,0},{4,5},{5,6},{6,7},{7,4},{8,9},{9,10},{10,1... | collective-permute-start | bytes 1179656 | tf_op jit(solution)/shard_map/ppermute | solution.py:17
  64.0 25.4 %slice-start.1 = ((s8[6291456]{0:T(1024)(128)(4,1)}), s8[2097152]{0:T(1024)(128)(4,1)S(1)}, s32[]{:S(2)}) async-start(s8[6291456]{0:T(1024)(128)(4,1)} %bitcast.65), calls=%async_computation.1 | async-start | bytes 4194304
  64.0 25.2 %collective-permute-start.10 = (bf16[48,4096]{1,0:T(8,128)(2,1)S(1)}, bf16[48,4096]{1,0:T(8,128)(2,1)S(1)}, u32[]{:S(2)}, u32[]{:S(2)}) collective-permute-start(bf16[48,4096]{1,0:T(8,128)(2,1)S(1)} %slice.266), channel_id=1, source_target_pairs={{0,3},{1,0},{2,1},{3,2},{4,7},{5,4},{6,5},{7,6},{8,11},{9,8},{10,9... | collective-permute-start | bytes 1179656 | tf_op jit(solution)/shard_map/ppermute | solution.py:17
  76.2 19.9 %collective-permute-start.22 = (bf16[48,4096]{1,0:T(8,128)(2,1)S(1)}, bf16[48,4096]{1,0:T(8,128)(2,1)S(1)}, u32[]{:S(2)}, u32[]{:S(2)}) collective-permute-start(bf16[48,4096]{1,0:T(8,128)(2,1)S(1)} %slice.284), channel_id=1, source_target_pairs={{0,1},{1,2},{2,3},{3,0},{4,5},{5,6},{6,7},{7,4},{8,9},{9,10},{10,1... | collective-permute-start | bytes 1179656 | tf_op jit(solution)/shard_map/ppermute | solution.py:17
  80.9 16.2 %collective-permute-start.24 = (bf16[48,4096]{1,0:T(8,128)(2,1)S(1)}, bf16[48,4096]{1,0:T(8,128)(2,1)S(1)}, u32[]{:S(2)}, u32[]{:S(2)}) collective-permute-start(bf16[48,4096]{1,0:T(8,128)(2,1)S(1)} %slice.285), channel_id=1, source_target_pairs={{0,3},{1,0},{2,1},{3,2},{4,7},{5,4},{6,5},{7,6},{8,11},{9,8},{10,9... | collective-permute-start | bytes 1179656 | tf_op jit(solution)/shard_map/ppermute | solution.py:17
  94.0 10.0 %collective-permute-start.11 = (bf16[48,4096]{1,0:T(8,128)(2,1)S(1)}, bf16[48,4096]{1,0:T(8,128)(2,1)S(1)}, u32[]{:S(2)}, u32[]{:S(2)}) collective-permute-start(bf16[48,4096]{1,0:T(8,128)(2,1)S(1)} %get-tuple-element.9), channel_id=1, source_target_pairs={{0,1},{1,2},{2,3},{3,0},{4,5},{5,6},{6,7},{7,4},{8,9},{9,10},{10,1... | collective-permute-start | bytes 1179656 | tf_op jit(solution)/shard_map/ppermute | solution.py:17
  94.1 11.7 %collective-permute-start.13 = (bf16[48,4096]{1,0:T(8,128)(2,1)S(1)}, bf16[48,4096]{1,0:T(8,128)(2,1)S(1)}, u32[]{:S(2)}, u32[]{:S(2)}) collective-permute-start(bf16[48,4096]{1,0:T(8,128)(2,1)S(1)} %get-tuple-element.10), channel_id=1, source_target_pairs={{0,3},{1,0},{2,1},{3,2},{4,7},{5,4},{6,5},{7,6},{8,11},{9,8},{10,9... | collective-permute-start | bytes 1179656 | tf_op jit(solution)/shard_map/ppermute | solution.py:17
  101.7 12.1 %collective-permute-start.25 = (bf16[48,4096]{1,0:T(8,128)(2,1)S(1)}, bf16[48,4096]{1,0:T(8,128)(2,1)S(1)}, u32[]{:S(2)}, u32[]{:S(2)}) collective-permute-start(bf16[48,4096]{1,0:T(8,128)(2,1)S(1)} %get-tuple-element.15), channel_id=1, source_target_pairs={{0,1},{1,2},{2,3},{3,0},{4,5},{5,6},{6,7},{7,4},{8,9},{9,10},{10,1... | collective-permute-start | bytes 1179656 | tf_op jit(solution)/shard_map/ppermute | solution.py:17
  102.4 13.3 %collective-permute-start.27 = (bf16[48,4096]{1,0:T(8,128)(2,1)S(1)}, bf16[48,4096]{1,0:T(8,128)(2,1)S(1)}, u32[]{:S(2)}, u32[]{:S(2)}) collective-permute-start(bf16[48,4096]{1,0:T(8,128)(2,1)S(1)} %get-tuple-element.16), channel_id=1, source_target_pairs={{0,3},{1,0},{2,1},{3,2},{4,7},{5,4},{6,5},{7,6},{8,11},{9,8},{10,9... | collective-permute-start | bytes 1179656 | tf_op jit(solution)/shard_map/ppermute | solution.py:17
  106.0 24.7 %collective-permute-start.12 = (bf16[96,4096]{1,0:T(8,128)(2,1)S(1)}, bf16[96,4096]{1,0:T(8,128)(2,1)S(1)}, u32[]{:S(2)}, u32[]{:S(2)}) collective-permute-start(bf16[96,4096]{1,0:T(8,128)(2,1)S(1)} %pad_maximum_fusion), channel_id=1, source_target_pairs={{0,1},{1,2},{2,3},{3,0},{4,5},{5,6},{6,7},{7,4},{8,9},{9,10},{10,1... | collective-permute-start | bytes 2359304 | tf_op jit(solution)/shard_map/ppermute | solution.py:17
  106.1 26.3 %collective-permute-start.14 = (bf16[96,4096]{1,0:T(8,128)(2,1)S(1)}, bf16[96,4096]{1,0:T(8,128)(2,1)S(1)}, u32[]{:S(2)}, u32[]{:S(2)}) collective-permute-start(bf16[96,4096]{1,0:T(8,128)(2,1)S(1)} %pad_maximum_fusion.1), channel_id=1, source_target_pairs={{0,3},{1,0},{2,1},{3,2},{4,7},{5,4},{6,5},{7,6},{8,11},{9,8},{10,9... | collective-permute-start | bytes 2359304 | tf_op jit(solution)/shard_map/ppermute | solution.py:17
  115.9 28.1 %collective-permute-start.26 = (bf16[96,4096]{1,0:T(8,128)(2,1)S(1)}, bf16[96,4096]{1,0:T(8,128)(2,1)S(1)}, u32[]{:S(2)}, u32[]{:S(2)}) collective-permute-start(bf16[96,4096]{1,0:T(8,128)(2,1)S(1)} %pad_maximum_fusion.2), channel_id=1, source_target_pairs={{0,1},{1,2},{2,3},{3,0},{4,5},{5,6},{6,7},{7,4},{8,9},{9,10},{10,1... | collective-permute-start | bytes 2359304 | tf_op jit(solution)/shard_map/ppermute | solution.py:17
  116.0 29.4 %collective-permute-start.28 = (bf16[96,4096]{1,0:T(8,128)(2,1)S(1)}, bf16[96,4096]{1,0:T(8,128)(2,1)S(1)}, u32[]{:S(2)}, u32[]{:S(2)}) collective-permute-start(bf16[96,4096]{1,0:T(8,128)(2,1)S(1)} %pad_maximum_fusion.3), channel_id=1, source_target_pairs={{0,3},{1,0},{2,1},{3,2},{4,7},{5,4},{6,5},{7,6},{8,11},{9,8},{10,9... | collective-permute-start | bytes 2359304 | tf_op jit(solution)/shard_map/ppermute | solution.py:17
  132.8 17.1 %collective-permute-start.15 = (bf16[24,4096]{1,0:T(8,128)(2,1)S(1)}, bf16[24,4096]{1,0:T(8,128)(2,1)S(1)}, u32[]{:S(2)}, u32[]{:S(2)}) collective-permute-start(bf16[24,4096]{1,0:T(8,128)(2,1)S(1)} %get-tuple-element.22), channel_id=1, source_target_pairs={{0,12},{1,13},{2,14},{3,15},{4,0},{5,1},{6,2},{7,3},{8,4},{9,5},{1... | collective-permute-start | bytes 589832 | tf_op jit(solution)/shard_map/ppermute | solution.py:22
  136.5 14.4 %collective-permute-start.16 = (bf16[24,4096]{1,0:T(8,128)(2,1)S(1)}, bf16[24,4096]{1,0:T(8,128)(2,1)S(1)}, u32[]{:S(2)}, u32[]{:S(2)}) collective-permute-start(bf16[24,4096]{1,0:T(8,128)(2,1)S(1)} %get-tuple-element.21), channel_id=1, source_target_pairs={{0,8},{1,9},{2,10},{3,11},{4,12},{5,13},{6,14},{7,15},{8,0},{9,1},... | collective-permute-start | bytes 589832 | tf_op jit(solution)/shard_map/ppermute | solution.py:22
  144.0 11.6 %collective-permute-start.17 = (bf16[24,4096]{1,0:T(8,128)(2,1)S(1)}, bf16[24,4096]{1,0:T(8,128)(2,1)S(1)}, u32[]{:S(2)}, u32[]{:S(2)}) collective-permute-start(bf16[24,4096]{1,0:T(8,128)(2,1)S(1)} %get-tuple-element.20), channel_id=1, source_target_pairs={{0,4},{1,5},{2,6},{3,7},{4,8},{5,9},{6,10},{7,11},{8,12},{9,13},{1... | collective-permute-start | bytes 589832 | tf_op jit(solution)/shard_map/ppermute | solution.py:22
  145.8 10.1 %collective-permute-start.29 = (bf16[24,4096]{1,0:T(8,128)(2,1)S(1)}, bf16[24,4096]{1,0:T(8,128)(2,1)S(1)}, u32[]{:S(2)}, u32[]{:S(2)}) collective-permute-start(bf16[24,4096]{1,0:T(8,128)(2,1)S(1)} %get-tuple-element.26), channel_id=1, source_target_pairs={{0,12},{1,13},{2,14},{3,15},{4,0},{5,1},{6,2},{7,3},{8,4},{9,5},{1... | collective-permute-start | bytes 589832 | tf_op jit(solution)/shard_map/ppermute | solution.py:22
  149.5 8.6 %collective-permute-start.30 = (bf16[24,4096]{1,0:T(8,128)(2,1)S(1)}, bf16[24,4096]{1,0:T(8,128)(2,1)S(1)}, u32[]{:S(2)}, u32[]{:S(2)}) collective-permute-start(bf16[24,4096]{1,0:T(8,128)(2,1)S(1)} %get-tuple-element.25), channel_id=1, source_target_pairs={{0,8},{1,9},{2,10},{3,11},{4,12},{5,13},{6,14},{7,15},{8,0},{9,1},... | collective-permute-start | bytes 589832 | tf_op jit(solution)/shard_map/ppermute | solution.py:22
  149.9 9.8 %collective-permute-start.31 = (bf16[24,4096]{1,0:T(8,128)(2,1)S(1)}, bf16[24,4096]{1,0:T(8,128)(2,1)S(1)}, u32[]{:S(2)}, u32[]{:S(2)}) collective-permute-start(bf16[24,4096]{1,0:T(8,128)(2,1)S(1)} %get-tuple-element.24), channel_id=1, source_target_pairs={{0,4},{1,5},{2,6},{3,7},{4,8},{5,9},{6,10},{7,11},{8,12},{9,13},{1... | collective-permute-start | bytes 589832 | tf_op jit(solution)/shard_map/ppermute | solution.py:22

commit v2 on v1

v2 whole, which is shorter than its diff:
```python
import jax
import jax.numpy as jnp
from jax import lax
from jax.experimental import pallas as pl
from jax.experimental.pallas import tpu as pltpu
from jax.sharding import PartitionSpec as P

SIDE = 4
F32, BF16 = jnp.float32, jnp.bfloat16


def shift_z(v, by):
    n = lax.axis_size("section")
    return lax.ppermute(v, "section", [(i, (i + by) % n) for i in range(n)])


def shift_x(v, by):
    pairs = [(i, i // SIDE * SIDE + (i + by) % SIDE) for i in range(SIDE * SIDE)]
    return lax.ppermute(v, "et", pairs)


def shift_y(v, by):
    n = SIDE * SIDE
    return lax.ppermute(v, "et", [(i, (i + SIDE * by) % n) for i in range(n)])


def gather_x(block):
    half = block.shape[0] // 2
    left, right = shift_x(block, 1), shift_x(block, -1)
    far = [shift_x(left[:half], 1), shift_x(right[half:], -1)]
    return [block, left, *far, right]


def scatter_sum_x(parts):
    half = parts[0].shape[0] // 2
    add = lambda a, b: (a.astype(F32) + b.astype(F32)).astype(BF16)
    to_right = shift_x(parts[2][:half], 1)
    to_left = shift_x(parts[2][half:], -1)
    right = jnp.concatenate([add(parts[3][:half], to_right), parts[3][half:]], 0)
    left = jnp.concatenate([parts[1][:half], add(parts[1][half:], to_left)], 0)
    from_left, from_right = shift_x(right, 1), shift_x(left, -1)
    return parts[0].astype(F32) + from_left.astype(F32) + from_right.astype(F32)


def slot_map(ids, row, cap):
    toks = ids.shape[0]
    same = (ids[:, None] == ids[None, :]) & (
        jnp.arange(toks)[:, None] > jnp.arange(toks)[None, :]
    )
    rank = jnp.sum(same.astype(jnp.int32), axis=1)
    target = (ids - row) % SIDE * cap + rank
    return (jnp.arange(SIDE * cap)[:, None] == target[None, :]).astype(BF16)


def whole(shape):
    return pl.BlockSpec(shape, lambda i: (0,) * len(shape))


def batch_of(shape, batch):
    return pl.BlockSpec((1, *shape[1:]), lambda i: (batch,) + (0,) * (len(shape) - 1))


def pack(rows, batch, gain, routing, row, cap, after):
    toks, width = rows.shape[1:]

    def kernel(base, a, g, r, *rest):
        outs = rest[len(after) :]
        i, j = (lax.broadcasted_iota(jnp.int32, (toks, toks), d) for d in range(2))
        across = jnp.broadcast_to(r[...], (toks, toks))
        down = jnp.sum(jnp.where(i == j, across, 0.0), 1, keepdims=True)
        earlier = jnp.where((across == down) & (j < i), 1.0, 0.0)
        rank = jnp.sum(earlier, 1, keepdims=True).astype(jnp.int32)
        target = lax.rem(down.astype(jnp.int32) - base[0] + SIDE, SIDE) * cap + rank
        slot = lax.broadcasted_iota(jnp.int32, (toks, SIDE * cap), 1)
        onehot = jnp.where(slot == target, 1.0, 0.0).astype(BF16)
        values = a[0].astype(F32)
        scale = lax.rsqrt(jnp.mean(values * values, axis=-1, keepdims=True) + 1e-06)
        normed = (values * scale * g[...]).astype(BF16)
        slots = lax.dot_general(
            onehot, normed, (((0,), (0,)), ((), ())), preferred_element_type=F32
        )
        for k in range(SIDE):
            outs[k][...] = slots[k * cap : (k + 1) * cap].astype(BF16)

    return pl.pallas_call(
        kernel,
        grid=(1,),
        out_shape=[jax.ShapeDtypeStruct((cap, width), BF16)] * SIDE,
        in_specs=[
            pl.BlockSpec(memory_space=pltpu.SMEM),
            batch_of(rows.shape, batch),
            whole(gain.shape),
            whole(routing.shape),
            *[pl.BlockSpec((16, 128), lambda i: (0, 0)) for _ in after],
        ],
        out_specs=[whole((cap, width))] * SIDE,
        compiler_params=pltpu.CompilerParams(vmem_limit_bytes=12 << 20),
        name="pack",
    )(row, rows, gain, routing, *after)


def finish(raw, batch, gate, onehot, back, earlier):
    toks, width = raw.shape[1:]

    def kernel(r, g, s, *rest):
        out = rest[-1]
        i, j = (lax.broadcasted_iota(jnp.int32, (toks, toks), d) for d in range(2))
        scale = jnp.sum(jnp.where(i == j, g[batch : batch + 1], 0.0), 1, keepdims=True)
        if earlier:
            out[:batch] = rest[SIDE][...]
        sums = sum(
            lax.dot_general(
                s[k], rest[k][...], (((0,), (0,)), ((), ())), preferred_element_type=F32
            )
            for k in range(SIDE)
        )
        out[batch] = (r[0].astype(F32) + scale * sums).astype(BF16)

    shape = (batch + 1, toks, width)
    return pl.pallas_call(
        kernel,
        grid=(1,),
        out_shape=jax.ShapeDtypeStruct(shape, BF16),
        in_specs=[
            batch_of(raw.shape, 0),
            *[whole(v.shape) for v in (gate, onehot, *back, *earlier)],
        ],
        out_specs=whole(shape),
        compiler_params=pltpu.CompilerParams(vmem_limit_bytes=16 << 20),
        name="finish",
    )(raw, gate, onehot, *back, *earlier)


def per_device(acts, expert_ids, gates, norm_gain, w_gate_up, w_down):
    _, batches, toks, width = acts.shape
    cap = min(toks, 3 * toks // (2 * SIDE))
    row = lax.axis_index("et") // SIDE
    ids = expert_ids[0, :, :, 0]
    arriving = [shift_z(acts[0, b : b + 1], 1) for b in range(batches)]
    mine = []
    for b in range(batches):
        routing = ids[b : b + 1].astype(F32)
        packed = pack(arriving[b], 0, norm_gain, routing, row[None], cap, mine)
        landed = [packed[0]] + [shift_y(packed[k], k) for k in range(1, SIDE)]
        mine.append(jnp.concatenate(landed, 0))

    hidden = []
    for b in range(batches):
        rows = jnp.concatenate(gather_x(mine[b]), 0)
        both = jnp.einsum("rd,dkf->rkf", rows, w_gate_up[0, 0], preferred_element_type=F32)
        hidden.append((jax.nn.silu(both[:, 0]) * both[:, 1]).astype(BF16))

    out = []
    for b in range(batches):
        part = jnp.dot(hidden[b], w_down[0, 0], preferred_element_type=F32).astype(BF16)
        part = part.reshape(SIDE, SIDE * cap, width)
        summed = scatter_sum_x([part[j] for j in range(SIDE)]).astype(BF16)
        summed = summed.reshape(SIDE, cap, width)
        back = [summed[0]] + [shift_y(summed[k], -k) for k in range(1, SIDE)]
        onehot = slot_map(ids[b], row, cap).reshape(SIDE, cap, toks)
        out = [finish(arriving[b], b, gates[0], onehot, back, out)]
    return out[0][None]


def solution(mesh):
    in_specs = (
        P(("dp", "section"), None, "et", None),
        P(("dp", "section"), None, "et", None),
        P(("dp", "section"), None, "et"),
        P(("dp", "section"), None),
        P(("dp", "section"), "et", None, None, None),
        P(("dp", "section"), "et", None, None),
    )
    out_specs = P(("dp", "section"), None, "et", None)
    return jax.shard_map(
        per_device, mesh=mesh, in_specs=in_specs, out_specs=out_specs, check_vma=False
    )
```

time: 161 us -> 155 us (0.963)
  Pallas kernels: 0 us -> 7.91 us
  matrix products: 15.1 us -> 9.08 us
  other arithmetic: 6.94 us -> 2.14 us
  waiting for transfers between devices: 92.7 us -> 88.5 us
    ppermute x8 -> x0, waiting for transfers between devices: 25.8 us -> none  [shift_zy(): return lax.ppermute(v, ('section', 'et'), pairs)]
    ppermute x2, waiting for transfers between devices: 0.01 us -> 14.2 us  [shift_z(): return lax.ppermute(v, 'section', [(i, (i + by) % n) for i in range(n)])]
    ppermute x6 -> x12, starting transfers between devices: 9.96 us -> 20.8 us  [shift_y(): return lax.ppermute(v, 'et', [(i, (i + SIDE * by) % n) for i in range(n)])]
    ppermute x8 -> x0, starting transfers between devices: 10.5 us -> none  [shift_zy(): return lax.ppermute(v, ('section', 'et'), pairs)]
    ppermute x6 -> x12, waiting for transfers between devices: 8.38 us -> 16.6 us  [shift_y(): return lax.ppermute(v, 'et', [(i, (i + SIDE * by) % n) for i in range(n)])]
    pallas_call x0 -> x4, Pallas kernels: none -> 7.91 us  [the longest x2 4.5 us: finish(): pl.pallas_call(kernel, grid=(1,), out_shape=jax.ShapeDtypeStruct(shape, B...]
    dot_general x10 -> x0, matrix products: 6.27 us -> none  [the longest x8 5.57 us: per_device(): jnp.dot(to_slots[k], normed, preferred_element_type=F32).astype(BF16)]
    ppermute x2, starting transfers between devices: 5.94 us -> 3.83 us  [shift_z(): return lax.ppermute(v, 'section', [(i, (i + by) % n) for i in range(n)])]
  transfers between devices with their start and end apart: 32 -> 30, of which waited for: 24 -> 21; matrix products, arithmetic and copies ran while one was open for 10% -> 8% of each run, Pallas kernels for 0% -> 3%
where the time goes in v2:
time: 155 us; the launch traced here: 154 us
  waiting for transfers between devices  88.5 us (57%)
  starting transfers between devices  42.1 us (27%)
  matrix products  9.08 us (6%)
  Pallas kernels  7.91 us (5%)
  local copies, waits for them, and re-layouts  4.18 us (3%)
  other arithmetic  2.14 us (1%)
    ppermute x16, waiting for transfers between devices, shift_x(): return lax.ppermute(v, 'et', pairs)  57.7 us
    ppermute x12, starting transfers between devices, shift_y(): return lax.ppermute(v, 'et', [(i, (i + SIDE * by) % n) for i in range(n)])  20.8 us
    ppermute x16, starting transfers between devices, shift_x(): return lax.ppermute(v, 'et', pairs)  17.5 us
    ppermute x12, waiting for transfers between devices, shift_y(): return lax.ppermute(v, 'et', [(i, (i + SIDE * by) % n) for i in range(n)])  16.6 us
    ppermute x2, waiting for transfers between devices, shift_z(): return lax.ppermute(v, 'section', [(i, (i + by) % n) for i in range(n)])  14.2 us
    dot_general x2, matrix products, per_device(): jnp.einsum('rd,dkf->rkf', rows, w_gate_up[0, 0], preferred_element_type=F32)  5.46 us
    pallas_call x2, Pallas kernels, finish(): pl.pallas_call(kernel, grid=(1,), out_shape=jax.ShapeDtypeStruct(shape, B...  4.5 us
    ppermute x2, starting transfers between devices, shift_z(): return lax.ppermute(v, 'section', [(i, (i + by) % n) for i in range(n)])  3.83 us
  transfers between devices with their start and end apart: 30, of which 21 were waited for; matrix products, arithmetic and copies ran while one was open for 8% of the time, Pallas kernels for 3%

profile of v2, /device:TPU:6, one launch (start us, length us, event | category | flops | bytes accessed | tf_op | source)
XLA Modules:
  0.0 154.3 jit_solution(9014101796656774249)
XLA Ops:
  0.0 2.4 %slice_bitcast_fusion = (bf16[1,64,4096]{2,1,0:T(8,128)(2,1)}, bf16[1,64,4096]{2,1,0:T(8,128)(2,1)}) fusion(bf16[1,2,64,4096]{3,2,1,0:T(8,128)(2,1)} %param.6), kind=kLoop, calls=%fused_computation.24 | loop fusion | bytes 2097152 | tf_op jit(solution)/shard_map/squeeze | solution.py:139
  2.4 1.9 %collective-permute-start.1 = (bf16[1,64,4096]{2,1,0:T(8,128)(2,1)}, bf16[1,64,4096]{2,1,0:T(8,128)(2,1)}, u32[]{:S(2)}, u32[]{:S(2)}) collective-permute-start(bf16[1,64,4096]{2,1,0:T(8,128)(2,1)} %get-tuple-element.33), channel_id=1, source_target_pairs={{0,16},{16,32},{32,48},{48,64},{64,80},{80,96},{96,112},{112,0},{1... | collective-permute-start | bytes 1572872 | tf_op jit(solution)/shard_map/ppermute | solution.py:14
  4.4 1.9 %collective-permute-start = (bf16[1,64,4096]{2,1,0:T(8,128)(2,1)}, bf16[1,64,4096]{2,1,0:T(8,128)(2,1)}, u32[]{:S(2)}, u32[]{:S(2)}) collective-permute-start(bf16[1,64,4096]{2,1,0:T(8,128)(2,1)} %get-tuple-element.34), channel_id=1, source_target_pairs={{0,16},{16,32},{32,48},{48,64},{64,80},{80,96},{96,112},{112,0},{1... | collective-permute-start | bytes 1572872 | tf_op jit(solution)/shard_map/ppermute | solution.py:14
  7.1 14.2 %collective-permute-done.1.a.r = bf16[1,64,4096]{2,1,0:T(8,128)(2,1)} collective-permute-done((bf16[1,64,4096]{2,1,0:T(8,128)(2,1)}, bf16[1,64,4096]{2,1,0:T(8,128)(2,1)}, u32[]{:S(2)}, u32[]{:S(2)}) %collective-permute-start.1) | collective-permute-done | bytes 524320 | tf_op jit(solution)/shard_map/ppermute | solution.py:14
  22.1 1.6 %pack.2 = (bf16[24,4096]{1,0:T(8,128)(2,1)S(1)}, bf16[24,4096]{1,0:T(8,128)(2,1)S(1)}, bf16[24,4096]{1,0:T(8,128)(2,1)S(1)}, bf16[24,4096]{1,0:T(8,128)(2,1)S(1)}) custom-call(s32[1]{0:T(128)} %bitcast.3.base, bf16[1,64,4096]{2,1,0:T(8,128)(2,1)} %collective-permute-done.1.a.r, f32[1,4096]{1,0:T(1,128)S(1)} %copy-done.1, f32[1,64]{1,0:T(1,128)S(1)} %get-tuple-element.65.r), custom_call_target="tpu_custom_call" | custom-call | tf_op jit(solution)/shard_map/pack/pallas_call | solution.py:85
  23.7 1.7 %collective-permute-start.2 = (bf16[24,4096]{1,0:T(8,128)(2,1)S(1)}, bf16[24,4096]{1,0:T(8,128)(2,1)S(1)}, u32[]{:S(2)}, u32[]{:S(2)}) collective-permute-start(bf16[24,4096]{1,0:T(8,128)(2,1)S(1)} %get-tuple-element.14), channel_id=1, source_target_pairs={{0,4},{1,5},{2,6},{3,7},{4,8},{5,9},{6,10},{7,11},{8,12},{9,13},{1... | collective-permute-start | bytes 589832 | tf_op jit(solution)/shard_map/ppermute | solution.py:24
  25.4 3.0 %collective-permute-start.3 = (bf16[24,4096]{1,0:T(8,128)(2,1)S(1)}, bf16[24,4096]{1,0:T(8,128)(2,1)S(1)}, u32[]{:S(2)}, u32[]{:S(2)}) collective-permute-start(bf16[24,4096]{1,0:T(8,128)(2,1)S(1)} %get-tuple-element.15), channel_id=1, source_target_pairs={{0,8},{1,9},{2,10},{3,11},{4,12},{5,13},{6,14},{7,15},{8,0},{9,1},... | collective-permute-start | bytes 589832 | tf_op jit(solution)/shard_map/ppermute | solution.py:24
  28.4 1.3 collective-permute-start.4
  29.8 2.7 %collective-permute-done.2 = bf16[24,4096]{1,0:T(8,128)(2,1)S(1)} collective-permute-done((bf16[24,4096]{1,0:T(8,128)(2,1)S(1)}, bf16[24,4096]{1,0:T(8,128)(2,1)S(1)}, u32[]{:S(2)}, u32[]{:S(2)}) %collective-permute-start.2) | collective-permute-done | bytes 196640 | tf_op jit(solution)/shard_map/ppermute | solution.py:24
  32.5 3.3 %collective-permute-done.3 = bf16[24,4096]{1,0:T(8,128)(2,1)S(1)} collective-permute-done((bf16[24,4096]{1,0:T(8,128)(2,1)S(1)}, bf16[24,4096]{1,0:T(8,128)(2,1)S(1)}, u32[]{:S(2)}, u32[]{:S(2)}) %collective-permute-start.3) | collective-permute-done | bytes 196640 | tf_op jit(solution)/shard_map/ppermute | solution.py:24
  36.4 1.5 collective-permute-start.21
  37.9 1.8 %pack.3 = (bf16[24,4096]{1,0:T(8,128)(2,1)S(1)}, bf16[24,4096]{1,0:T(8,128)(2,1)S(1)}, bf16[24,4096]{1,0:T(8,128)(2,1)S(1)}, bf16[24,4096]{1,0:T(8,128)(2,1)S(1)}) custom-call(s32[1]{0:T(128)} %bitcast.3.base, bf16[1,64,4096]{2,1,0:T(8,128)(2,1)} %collective-permute-done.a.r, f32[1,4096]{1,0:T(1,128)S(1)} %copy-done.2, f32[1,64]{1,0:T(1,128)S(1)} %get-tuple-element.64.r, ...), custom_call_target="tpu_custom_call" | custom-call | tf_op jit(solution)/shard_map/pack/pallas_call | solution.py:85
  39.7 1.3 collective-permute-start.5
  41.1 2.5 %collective-permute-start.6 = (bf16[24,4096]{1,0:T(8,128)(2,1)S(1)}, bf16[24,4096]{1,0:T(8,128)(2,1)S(1)}, u32[]{:S(2)}, u32[]{:S(2)}) collective-permute-start(bf16[24,4096]{1,0:T(8,128)(2,1)S(1)} %get-tuple-element.19), channel_id=1, source_target_pairs={{0,8},{1,9},{2,10},{3,11},{4,12},{5,13},{6,14},{7,15},{8,0},{9,1},... | collective-permute-start | bytes 589832 | tf_op jit(solution)/shard_map/ppermute | solution.py:24
  43.5 1.7 %collective-permute-start.7 = (bf16[24,4096]{1,0:T(8,128)(2,1)S(1)}, bf16[24,4096]{1,0:T(8,128)(2,1)S(1)}, u32[]{:S(2)}, u32[]{:S(2)}) collective-permute-start(bf16[24,4096]{1,0:T(8,128)(2,1)S(1)} %get-tuple-element.20), channel_id=1, source_target_pairs={{0,12},{1,13},{2,14},{3,15},{4,0},{5,1},{6,2},{7,3},{8,4},{9,5},{1... | collective-permute-start | bytes 589832 | tf_op jit(solution)/shard_map/ppermute | solution.py:24
  45.2 2.8 %collective-permute-done.5 = bf16[24,4096]{1,0:T(8,128)(2,1)S(1)} collective-permute-done((bf16[24,4096]{1,0:T(8,128)(2,1)S(1)}, bf16[24,4096]{1,0:T(8,128)(2,1)S(1)}, u32[]{:S(2)}, u32[]{:S(2)}) %collective-permute-start.5) | collective-permute-done | bytes 196640 | tf_op jit(solution)/shard_map/ppermute | solution.py:24
  48.0 2.1 %collective-permute-done.6 = bf16[24,4096]{1,0:T(8,128)(2,1)S(1)} collective-permute-done((bf16[24,4096]{1,0:T(8,128)(2,1)S(1)}, bf16[24,4096]{1,0:T(8,128)(2,1)S(1)}, u32[]{:S(2)}, u32[]{:S(2)}) %collective-permute-start.6) | collective-permute-done | bytes 196640 | tf_op jit(solution)/shard_map/ppermute | solution.py:24
  50.2 1.8 %collective-permute-start.8 = (bf16[96,4096]{1,0:T(8,128)(2,1)S(1)}, bf16[96,4096]{1,0:T(8,128)(2,1)S(1)}, u32[]{:S(2)}, u32[]{:S(2)}) collective-permute-start(bf16[96,4096]{1,0:T(8,128)(2,1)S(1)} %get-tuple-element.51), channel_id=1, source_target_pairs={{0,1},{1,2},{2,3},{3,0},{4,5},{5,6},{6,7},{7,4},{8,9},{9,10},{10,1... | collective-permute-start | bytes 2359304 | tf_op jit(solution)/shard_map/ppermute | solution.py:19
  52.3 3.5 %collective-permute-done.19 = bf16[96,4096]{1,0:T(8,128)(2,1)S(1)} collective-permute-done((bf16[96,4096]{1,0:T(8,128)(2,1)S(1)}, bf16[96,4096]{1,0:T(8,128)(2,1)S(1)}, u32[]{:S(2)}, u32[]{:S(2)}) %collective-permute-start.19) | collective-permute-done | bytes 786464 | tf_op jit(solution)/shard_map/ppermute | solution.py:19
  56.4 1.6 %collective-permute-start.22 = (bf16[48,4096]{1,0:T(8,128)(2,1)S(1)}, bf16[48,4096]{1,0:T(8,128)(2,1)S(1)}, u32[]{:S(2)}, u32[]{:S(2)}) collective-permute-start(bf16[48,4096]{1,0:T(8,128)(2,1)S(1)} %slice.199), channel_id=1, source_target_pairs={{0,3},{1,0},{2,1},{3,2},{4,7},{5,4},{6,5},{7,6},{8,11},{9,8},{10,9... | collective-permute-start | bytes 1179656 | tf_op jit(solution)/shard_map/ppermute | solution.py:19
  58.1 14.5 %collective-permute-done.8 = bf16[96,4096]{1,0:T(8,128)(2,1)S(1)} collective-permute-done((bf16[96,4096]{1,0:T(8,128)(2,1)S(1)}, bf16[96,4096]{1,0:T(8,128)(2,1)S(1)}, u32[]{:S(2)}, u32[]{:S(2)}) %collective-permute-start.8) | collective-permute-done | bytes 786464 | tf_op jit(solution)/shard_map/ppermute | solution.py:19
  72.6 1.3 collective-permute-start.9
  74.0 1.1 collective-permute-start.11
  75.1 5.9 %collective-permute-done.20 = bf16[48,4096]{1,0:T(8,128)(2,1)S(1)} collective-permute-done((bf16[48,4096]{1,0:T(8,128)(2,1)S(1)}, bf16[48,4096]{1,0:T(8,128)(2,1)S(1)}, u32[]{:S(2)}, u32[]{:S(2)}) %collective-permute-start.20) | collective-permute-done | bytes 393248 | tf_op jit(solution)/shard_map/ppermute | solution.py:19
  82.2 2.7 %fusion = f32[384,2,384]{2,0,1:T(8,128)S(1)} fusion(bf16[4096,2,384]{2,1,0:T(2,128)(2,1)S(1)} %bitcast.41, bf16[384,4096]{1,0:T(8,128)(2,1)S(1)} %constant_dynamic-update-slice_fusion.16), kind=kOutput, calls=%fused_computation.2 | convolution fusion | flops 2415919104 | bytes 10616832 | tf_op jit(solution)/shard_map/rd,dkf->rkf/dot_general | solution.py:150
  84.9 1.8 %convolution_convert_fusion = bf16[384,4096]{1,0:T(8,128)(2,1)S(1)} fusion(bf16[1,1,384,4096]{3,2,1,0:T(8,128)(2,1)S(1)} %copy-done, f32[384,2,384]{2,0,1:T(8,128)S(1)} %fusion), kind=kOutput, calls=%fused_computation | convolution fusion | flops 1210417152 | bytes 7471104 | tf_op jit(solution)/shard_map/dot_general | solution.py:155
  87.5 1.5 collective-permute-start.25
  89.8 2.7 %fusion.2 = f32[384,2,384]{2,0,1:T(8,128)S(1)} fusion(bf16[4096,2,384]{2,1,0:T(2,128)(2,1)S(1)} %bitcast.42, bf16[384,4096]{1,0:T(8,128)(2,1)S(1)} %constant_dynamic-update-slice_fusion.8), kind=kOutput, calls=%fused_computation.4 | convolution fusion | flops 2415919104 | bytes 10616832 | tf_op jit(solution)/shard_map/rd,dkf->rkf/dot_general | solution.py:150
  92.5 1.8 %convolution_convert_fusion.1 = bf16[384,4096]{1,0:T(8,128)(2,1)S(1)} fusion(bf16[1,1,384,4096]{3,2,1,0:T(8,128)(2,1)S(1)} %copy-done, f32[384,2,384]{2,0,1:T(8,128)S(1)} %fusion.2), kind=kOutput, calls=%fused_computation.1 | convolution fusion | flops 1210417152 | bytes 7471104 | tf_op jit(solution)/shard_map/dot_general | solution.py:155
  94.5 1.2 collective-permute-start.12
  97.0 2.0 %collective-permute-done.25 = bf16[48,4096]{1,0:T(8,128)(2,1)S(1)} collective-permute-done((bf16[48,4096]{1,0:T(8,128)(2,1)S(1)}, bf16[48,4096]{1,0:T(8,128)(2,1)S(1)}, u32[]{:S(2)}, u32[]{:S(2)}) %collective-permute-start.25) | collective-permute-done | bytes 393248 | tf_op jit(solution)/shard_map/ppermute | solution.py:19
  99.2 1.7 %collective-permute-start.24 = (bf16[96,4096]{1,0:T(8,128)(2,1)S(1)}, bf16[96,4096]{1,0:T(8,128)(2,1)S(1)}, u32[]{:S(2)}, u32[]{:S(2)}) collective-permute-start(bf16[96,4096]{1,0:T(8,128)(2,1)S(1)} %pad_maximum_fusion.2), channel_id=1, source_target_pairs={{0,1},{1,2},{2,3},{3,0},{4,5},{5,6},{6,7},{7,4},{8,9},{9,10},{10,1... | collective-permute-start | bytes 2359304 | tf_op jit(solution)/shard_map/ppermute | solution.py:19
  101.7 4.9 %collective-permute-done.12 = bf16[48,4096]{1,0:T(8,128)(2,1)S(1)} collective-permute-done((bf16[48,4096]{1,0:T(8,128)(2,1)S(1)}, bf16[48,4096]{1,0:T(8,128)(2,1)S(1)}, u32[]{:S(2)}, u32[]{:S(2)}) %collective-permute-start.12) | collective-permute-done | bytes 393248 | tf_op jit(solution)/shard_map/ppermute | solution.py:19
  106.6 2.3 %collective-permute-done.14 = bf16[48,4096]{1,0:T(8,128)(2,1)S(1)} collective-permute-done((bf16[48,4096]{1,0:T(8,128)(2,1)S(1)}, bf16[48,4096]{1,0:T(8,128)(2,1)S(1)}, u32[]{:S(2)}, u32[]{:S(2)}) %collective-permute-start.14) | collective-permute-done | bytes 393248 | tf_op jit(solution)/shard_map/ppermute | solution.py:19
  109.3 2.1 %collective-permute-start.15 = (bf16[96,4096]{1,0:T(8,128)(2,1)S(1)}, bf16[96,4096]{1,0:T(8,128)(2,1)S(1)}, u32[]{:S(2)}, u32[]{:S(2)}) collective-permute-start(bf16[96,4096]{1,0:T(8,128)(2,1)S(1)} %pad_maximum_fusion.1), channel_id=1, source_target_pairs={{0,3},{1,0},{2,1},{3,2},{4,7},{5,4},{6,5},{7,6},{8,11},{9,8},{10,9... | collective-permute-start | bytes 2359304 | tf_op jit(solution)/shard_map/ppermute | solution.py:19
  111.4 12.0 %collective-permute-done.24 = bf16[96,4096]{1,0:T(8,128)(2,1)S(1)} collective-permute-done((bf16[96,4096]{1,0:T(8,128)(2,1)S(1)}, bf16[96,4096]{1,0:T(8,128)(2,1)S(1)}, u32[]{:S(2)}, u32[]{:S(2)}) %collective-permute-start.24) | collective-permute-done | bytes 786464 | tf_op jit(solution)/shard_map/ppermute | solution.py:19
  123.5 2.3 %collective-permute-done.26 = bf16[96,4096]{1,0:T(8,128)(2,1)S(1)} collective-permute-done((bf16[96,4096]{1,0:T(8,128)(2,1)S(1)}, bf16[96,4096]{1,0:T(8,128)(2,1)S(1)}, u32[]{:S(2)}, u32[]{:S(2)}) %collective-permute-start.26) | collective-permute-done | bytes 786464 | tf_op jit(solution)/shard_map/ppermute | solution.py:19
  126.1 3.2 %collective-permute-start.27 = (bf16[24,4096]{1,0:T(8,128)(2,1)S(1)}, bf16[24,4096]{1,0:T(8,128)(2,1)S(1)}, u32[]{:S(2)}, u32[]{:S(2)}) collective-permute-start(bf16[24,4096]{1,0:T(8,128)(2,1)S(1)} %get-tuple-element.37), channel_id=1, source_target_pairs={{0,12},{1,13},{2,14},{3,15},{4,0},{5,1},{6,2},{7,3},{8,4},{9,5},{1... | collective-permute-start | bytes 589832 | tf_op jit(solution)/shard_map/ppermute | solution.py:24
  129.4 1.2 collective-permute-start.28
  130.5 6.4 %collective-permute-done.13 = bf16[96,4096]{1,0:T(8,128)(2,1)S(1)} collective-permute-done((bf16[96,4096]{1,0:T(8,128)(2,1)S(1)}, bf16[96,4096]{1,0:T(8,128)(2,1)S(1)}, u32[]{:S(2)}, u32[]{:S(2)}) %collective-permute-start.13) | collective-permute-done | bytes 786464 | tf_op jit(solution)/shard_map/ppermute | solution.py:19
  136.9 1.7 %collective-permute-done.15 = bf16[96,4096]{1,0:T(8,128)(2,1)S(1)} collective-permute-done((bf16[96,4096]{1,0:T(8,128)(2,1)S(1)}, bf16[96,4096]{1,0:T(8,128)(2,1)S(1)}, u32[]{:S(2)}, u32[]{:S(2)}) %collective-permute-start.15) | collective-permute-done | bytes 786464 | tf_op jit(solution)/shard_map/ppermute | solution.py:19
  139.0 3.2 %collective-permute-start.16 = (bf16[24,4096]{1,0:T(8,128)(2,1)S(1)}, bf16[24,4096]{1,0:T(8,128)(2,1)S(1)}, u32[]{:S(2)}, u32[]{:S(2)}) collective-permute-start(bf16[24,4096]{1,0:T(8,128)(2,1)S(1)} %get-tuple-element.41), channel_id=1, source_target_pairs={{0,12},{1,13},{2,14},{3,15},{4,0},{5,1},{6,2},{7,3},{8,4},{9,5},{1... | collective-permute-start | bytes 589832 | tf_op jit(solution)/shard_map/ppermute | solution.py:24
  142.3 1.7 %collective-permute-start.17 = (bf16[24,4096]{1,0:T(8,128)(2,1)S(1)}, bf16[24,4096]{1,0:T(8,128)(2,1)S(1)}, u32[]{:S(2)}, u32[]{:S(2)}) collective-permute-start(bf16[24,4096]{1,0:T(8,128)(2,1)S(1)} %get-tuple-element.40), channel_id=1, source_target_pairs={{0,8},{1,9},{2,10},{3,11},{4,12},{5,13},{6,14},{7,15},{8,0},{9,1},... | collective-permute-start | bytes 589832 | tf_op jit(solution)/shard_map/ppermute | solution.py:24
  144.1 1.8 %finish.2.rest_4_ = bf16[1,64,4096]{2,1,0:T(8,128)(2,1)S(1)} custom-call(bf16[1,64,4096]{2,1,0:T(8,128)(2,1)} %collective-permute-done.1.a.r, f32[2,64]{1,0:T(2,128)S(1)} %bitcast.37, bf16[4,24,64]{2,1,0:T(8,128)(2,1)S(1)} %get-tuple-element.59.s, bf16[24,4096]{1,0:T(8,128)(2,1)S(1)} %get-tuple-element.38.rest_0_, ...), custom_call_target="tpu_custom_call" | custom-call | tf_op jit(solution)/shard_map/finish/pallas_call | solution.py:120
  145.8 1.8 %collective-permute-done.16.rest_1_ = bf16[24,4096]{1,0:T(8,128)(2,1)S(1)} collective-permute-done((bf16[24,4096]{1,0:T(8,128)(2,1)S(1)}, bf16[24,4096]{1,0:T(8,128)(2,1)S(1)}, u32[]{:S(2)}, u32[]{:S(2)}) %collective-permute-start.16) | collective-permute-done | bytes 196640 | tf_op jit(solution)/shard_map/ppermute | solution.py:24
  147.6 1.9 %collective-permute-done.17.rest_2_ = bf16[24,4096]{1,0:T(8,128)(2,1)S(1)} collective-permute-done((bf16[24,4096]{1,0:T(8,128)(2,1)S(1)}, bf16[24,4096]{1,0:T(8,128)(2,1)S(1)}, u32[]{:S(2)}, u32[]{:S(2)}) %collective-permute-start.17) | collective-permute-done | bytes 196640 | tf_op jit(solution)/shard_map/ppermute | solution.py:24
  149.5 2.0 %collective-permute-done.18.rest_3_ = bf16[24,4096]{1,0:T(8,128)(2,1)S(1)} collective-permute-done((bf16[24,4096]{1,0:T(8,128)(2,1)S(1)}, bf16[24,4096]{1,0:T(8,128)(2,1)S(1)}, u32[]{:S(2)}, u32[]{:S(2)}) %collective-permute-start.18) | collective-permute-done | bytes 196640 | tf_op jit(solution)/shard_map/ppermute | solution.py:24
  151.5 2.7 %finish.3 = bf16[2,64,4096]{2,1,0:T(8,128)(2,1)} custom-call(bf16[1,64,4096]{2,1,0:T(8,128)(2,1)} %collective-permute-done.a.r, f32[2,64]{1,0:T(2,128)S(1)} %bitcast.38, bf16[4,24,64]{2,1,0:T(8,128)(2,1)S(1)} %get-tuple-element.60.s, bf16[24,4096]{1,0:T(8,128)(2,1)S(1)} %get-tuple-element.42.rest_0_, bf16[24,4096]{1,0:T(8,128)(2,1)S(1)} %collective-permute-done.16.rest_1_, ...), custom_call_target="tpu_custom_call" | custom-call | tf_op jit(solution)/shard_map/finish/pallas_call | solution.py:120
  (73 shorter events, 9.8 us)
Async XLA Ops:
  0.0 84.9 %copy-start = (bf16[1,1,384,4096]{3,2,1,0:T(8,128)(2,1)S(1)}, bf16[1,1,384,4096]{3,2,1,0:T(8,128)(2,1)}, u32[]{:S(2)}) copy-start(bf16[1,1,384,4096]{3,2,1,0:T(8,128)(2,1)} %param.11) | copy-start | bytes 9437188
  0.0 37.9 %copy-start.2 = (f32[1,4096]{1,0:T(1,128)S(1)}, f32[1,4096]{1,0:T(1,128)}, u32[]{:S(2)}) copy-start(f32[1,4096]{1,0:T(1,128)} %g.3) | copy-start | bytes 49156
  2.4 18.9 %collective-permute-start.1 = (bf16[1,64,4096]{2,1,0:T(8,128)(2,1)}, bf16[1,64,4096]{2,1,0:T(8,128)(2,1)}, u32[]{:S(2)}, u32[]{:S(2)}) collective-permute-start(bf16[1,64,4096]{2,1,0:T(8,128)(2,1)} %get-tuple-element.33), channel_id=1, source_target_pairs={{0,16},{16,32},{32,48},{48,64},{64,80},{80,96},{96,112},{112,0},{1... | collective-permute-start | bytes 1572872 | tf_op jit(solution)/shard_map/ppermute | solution.py:14
  4.4 33.6 %collective-permute-start = (bf16[1,64,4096]{2,1,0:T(8,128)(2,1)}, bf16[1,64,4096]{2,1,0:T(8,128)(2,1)}, u32[]{:S(2)}, u32[]{:S(2)}) collective-permute-start(bf16[1,64,4096]{2,1,0:T(8,128)(2,1)} %get-tuple-element.34), channel_id=1, source_target_pairs={{0,16},{16,32},{32,48},{48,64},{64,80},{80,96},{96,112},{112,0},{1... | collective-permute-start | bytes 1572872 | tf_op jit(solution)/shard_map/ppermute | solution.py:14
  21.4 0.7 copy-start.1
  23.7 28.6 %copy-start.4 = (s32[1,2,64,1]{2,3,1,0:T(1,128)S(1)}, s32[1,2,64,1]{2,3,1,0:T(1,128)}, u32[]{:S(2)}) copy-start(s32[1,2,64,1]{2,3,1,0:T(1,128)} %param.7) | copy-start | bytes 1540
  23.7 8.7 %collective-permute-start.2 = (bf16[24,4096]{1,0:T(8,128)(2,1)S(1)}, bf16[24,4096]{1,0:T(8,128)(2,1)S(1)}, u32[]{:S(2)}, u32[]{:S(2)}) collective-permute-start(bf16[24,4096]{1,0:T(8,128)(2,1)S(1)} %get-tuple-element.14), channel_id=1, source_target_pairs={{0,4},{1,5},{2,6},{3,7},{4,8},{5,9},{6,10},{7,11},{8,12},{9,13},{1... | collective-permute-start | bytes 589832 | tf_op jit(solution)/shard_map/ppermute | solution.py:24
  25.4 10.3 %collective-permute-start.3 = (bf16[24,4096]{1,0:T(8,128)(2,1)S(1)}, bf16[24,4096]{1,0:T(8,128)(2,1)S(1)}, u32[]{:S(2)}, u32[]{:S(2)}) collective-permute-start(bf16[24,4096]{1,0:T(8,128)(2,1)S(1)} %get-tuple-element.15), channel_id=1, source_target_pairs={{0,8},{1,9},{2,10},{3,11},{4,12},{5,13},{6,14},{7,15},{8,0},{9,1},... | collective-permute-start | bytes 589832 | tf_op jit(solution)/shard_map/ppermute | solution.py:24
  28.4 7.4 %collective-permute-start.4 = (bf16[24,4096]{1,0:T(8,128)(2,1)S(1)}, bf16[24,4096]{1,0:T(8,128)(2,1)S(1)}, u32[]{:S(2)}, u32[]{:S(2)}) collective-permute-start(bf16[24,4096]{1,0:T(8,128)(2,1)S(1)} %get-tuple-element.16), channel_id=1, source_target_pairs={{0,12},{1,13},{2,14},{3,15},{4,0},{5,1},{6,2},{7,3},{8,4},{9,5},{1... | collective-permute-start | bytes 589832 | tf_op jit(solution)/shard_map/ppermute | solution.py:24
  35.8 19.9 %collective-permute-start.19 = (bf16[96,4096]{1,0:T(8,128)(2,1)S(1)}, bf16[96,4096]{1,0:T(8,128)(2,1)S(1)}, u32[]{:S(2)}, u32[]{:S(2)}) collective-permute-start(bf16[96,4096]{1,0:T(8,128)(2,1)S(1)} %get-tuple-element.44.rest_0_), channel_id=1, source_target_pairs={{0,1},{1,2},{2,3},{3,0},{4,5},{5,6},{6,7},{7,4},{8,9},{9,10},{10,1... | collective-permute-start | bytes 2359304 | tf_op jit(solution)/shard_map/ppermute | solution.py:19
  36.4 20.0 %collective-permute-start.21 = (bf16[96,4096]{1,0:T(8,128)(2,1)S(1)}, bf16[96,4096]{1,0:T(8,128)(2,1)S(1)}, u32[]{:S(2)}, u32[]{:S(2)}) collective-permute-start(bf16[96,4096]{1,0:T(8,128)(2,1)S(1)} %get-tuple-element.44.rest_0_), channel_id=1, source_target_pairs={{0,3},{1,0},{2,1},{3,2},{4,7},{5,4},{6,5},{7,6},{8,11},{9,8},{10,9... | collective-permute-start | bytes 2359304 | tf_op jit(solution)/shard_map/ppermute | solution.py:19
  37.9 44.2 %slice-start = ((s8[6291456]{0:T(1024)(128)(4,1)}), s8[4194304]{0:T(1024)(128)(4,1)S(1)}, s32[]{:S(2)}) async-start(s8[6291456]{0:T(1024)(128)(4,1)} %bitcast.39), calls=%async_computation | async-start | bytes 8388608
  39.7 8.3 %collective-permute-start.5 = (bf16[24,4096]{1,0:T(8,128)(2,1)S(1)}, bf16[24,4096]{1,0:T(8,128)(2,1)S(1)}, u32[]{:S(2)}, u32[]{:S(2)}) collective-permute-start(bf16[24,4096]{1,0:T(8,128)(2,1)S(1)} %get-tuple-element.18), channel_id=1, source_target_pairs={{0,4},{1,5},{2,6},{3,7},{4,8},{5,9},{6,10},{7,11},{8,12},{9,13},{1... | collective-permute-start | bytes 589832 | tf_op jit(solution)/shard_map/ppermute | solution.py:24
  41.1 9.0 %collective-permute-start.6 = (bf16[24,4096]{1,0:T(8,128)(2,1)S(1)}, bf16[24,4096]{1,0:T(8,128)(2,1)S(1)}, u32[]{:S(2)}, u32[]{:S(2)}) collective-permute-start(bf16[24,4096]{1,0:T(8,128)(2,1)S(1)} %get-tuple-element.19), channel_id=1, source_target_pairs={{0,8},{1,9},{2,10},{3,11},{4,12},{5,13},{6,14},{7,15},{8,0},{9,1},... | collective-permute-start | bytes 589832 | tf_op jit(solution)/shard_map/ppermute | solution.py:24
  43.5 6.6 %collective-permute-start.7 = (bf16[24,4096]{1,0:T(8,128)(2,1)S(1)}, bf16[24,4096]{1,0:T(8,128)(2,1)S(1)}, u32[]{:S(2)}, u32[]{:S(2)}) collective-permute-start(bf16[24,4096]{1,0:T(8,128)(2,1)S(1)} %get-tuple-element.20), channel_id=1, source_target_pairs={{0,12},{1,13},{2,14},{3,15},{4,0},{5,1},{6,2},{7,3},{8,4},{9,5},{1... | collective-permute-start | bytes 589832 | tf_op jit(solution)/shard_map/ppermute | solution.py:24
  50.2 22.4 %collective-permute-start.8 = (bf16[96,4096]{1,0:T(8,128)(2,1)S(1)}, bf16[96,4096]{1,0:T(8,128)(2,1)S(1)}, u32[]{:S(2)}, u32[]{:S(2)}) collective-permute-start(bf16[96,4096]{1,0:T(8,128)(2,1)S(1)} %get-tuple-element.51), channel_id=1, source_target_pairs={{0,1},{1,2},{2,3},{3,0},{4,5},{5,6},{6,7},{7,4},{8,9},{9,10},{10,1... | collective-permute-start | bytes 2359304 | tf_op jit(solution)/shard_map/ppermute | solution.py:19
  52.0 22.0 %collective-permute-start.10 = (bf16[96,4096]{1,0:T(8,128)(2,1)S(1)}, bf16[96,4096]{1,0:T(8,128)(2,1)S(1)}, u32[]{:S(2)}, u32[]{:S(2)}) collective-permute-start(bf16[96,4096]{1,0:T(8,128)(2,1)S(1)} %get-tuple-element.51), channel_id=1, source_target_pairs={{0,3},{1,0},{2,1},{3,2},{4,7},{5,4},{6,5},{7,6},{8,11},{9,8},{10,9... | collective-permute-start | bytes 2359304 | tf_op jit(solution)/shard_map/ppermute | solution.py:19
  55.8 25.2 %collective-permute-start.20 = (bf16[48,4096]{1,0:T(8,128)(2,1)S(1)}, bf16[48,4096]{1,0:T(8,128)(2,1)S(1)}, u32[]{:S(2)}, u32[]{:S(2)}) collective-permute-start(bf16[48,4096]{1,0:T(8,128)(2,1)S(1)} %slice.198), channel_id=1, source_target_pairs={{0,1},{1,2},{2,3},{3,0},{4,5},{5,6},{6,7},{7,4},{8,9},{9,10},{10,1... | collective-permute-start | bytes 1179656 | tf_op jit(solution)/shard_map/ppermute | solution.py:19
  56.4 25.7 %collective-permute-start.22 = (bf16[48,4096]{1,0:T(8,128)(2,1)S(1)}, bf16[48,4096]{1,0:T(8,128)(2,1)S(1)}, u32[]{:S(2)}, u32[]{:S(2)}) collective-permute-start(bf16[48,4096]{1,0:T(8,128)(2,1)S(1)} %slice.199), channel_id=1, source_target_pairs={{0,3},{1,0},{2,1},{3,2},{4,7},{5,4},{6,5},{7,6},{8,11},{9,8},{10,9... | collective-permute-start | bytes 1179656 | tf_op jit(solution)/shard_map/ppermute | solution.py:19
  58.0 24.2 %slice-start.1 = ((s8[6291456]{0:T(1024)(128)(4,1)}), s8[2097152]{0:T(1024)(128)(4,1)S(1)}, s32[]{:S(2)}) async-start(s8[6291456]{0:T(1024)(128)(4,1)} %bitcast.39), calls=%async_computation.1 | async-start | bytes 4194304
  72.6 16.4 %collective-permute-start.9 = (bf16[48,4096]{1,0:T(8,128)(2,1)S(1)}, bf16[48,4096]{1,0:T(8,128)(2,1)S(1)}, u32[]{:S(2)}, u32[]{:S(2)}) collective-permute-start(bf16[48,4096]{1,0:T(8,128)(2,1)S(1)} %slice.183), channel_id=1, source_target_pairs={{0,1},{1,2},{2,3},{3,0},{4,5},{5,6},{6,7},{7,4},{8,9},{9,10},{10,1... | collective-permute-start | bytes 1179656 | tf_op jit(solution)/shard_map/ppermute | solution.py:19
  74.0 15.7 %collective-permute-start.11 = (bf16[48,4096]{1,0:T(8,128)(2,1)S(1)}, bf16[48,4096]{1,0:T(8,128)(2,1)S(1)}, u32[]{:S(2)}, u32[]{:S(2)}) collective-permute-start(bf16[48,4096]{1,0:T(8,128)(2,1)S(1)} %slice.184), channel_id=1, source_target_pairs={{0,3},{1,0},{2,1},{3,2},{4,7},{5,4},{6,5},{7,6},{8,11},{9,8},{10,9... | collective-permute-start | bytes 1179656 | tf_op jit(solution)/shard_map/ppermute | solution.py:19
  86.9 10.1 %collective-permute-start.23 = (bf16[48,4096]{1,0:T(8,128)(2,1)S(1)}, bf16[48,4096]{1,0:T(8,128)(2,1)S(1)}, u32[]{:S(2)}, u32[]{:S(2)}) collective-permute-start(bf16[48,4096]{1,0:T(8,128)(2,1)S(1)} %get-tuple-element.23), channel_id=1, source_target_pairs={{0,1},{1,2},{2,3},{3,0},{4,5},{5,6},{6,7},{7,4},{8,9},{9,10},{10,1... | collective-permute-start | bytes 1179656 | tf_op jit(solution)/shard_map/ppermute | solution.py:19
  87.5 11.4 %collective-permute-start.25 = (bf16[48,4096]{1,0:T(8,128)(2,1)S(1)}, bf16[48,4096]{1,0:T(8,128)(2,1)S(1)}, u32[]{:S(2)}, u32[]{:S(2)}) collective-permute-start(bf16[48,4096]{1,0:T(8,128)(2,1)S(1)} %get-tuple-element.24), channel_id=1, source_target_pairs={{0,3},{1,0},{2,1},{3,2},{4,7},{5,4},{6,5},{7,6},{8,11},{9,8},{10,9... | collective-permute-start | bytes 1179656 | tf_op jit(solution)/shard_map/ppermute | solution.py:19
  94.5 12.1 %collective-permute-start.12 = (bf16[48,4096]{1,0:T(8,128)(2,1)S(1)}, bf16[48,4096]{1,0:T(8,128)(2,1)S(1)}, u32[]{:S(2)}, u32[]{:S(2)}) collective-permute-start(bf16[48,4096]{1,0:T(8,128)(2,1)S(1)} %get-tuple-element.29), channel_id=1, source_target_pairs={{0,1},{1,2},{2,3},{3,0},{4,5},{5,6},{6,7},{7,4},{8,9},{9,10},{10,1... | collective-permute-start | bytes 1179656 | tf_op jit(solution)/shard_map/ppermute | solution.py:19
  95.7 13.3 %collective-permute-start.14 = (bf16[48,4096]{1,0:T(8,128)(2,1)S(1)}, bf16[48,4096]{1,0:T(8,128)(2,1)S(1)}, u32[]{:S(2)}, u32[]{:S(2)}) collective-permute-start(bf16[48,4096]{1,0:T(8,128)(2,1)S(1)} %get-tuple-element.30), channel_id=1, source_target_pairs={{0,3},{1,0},{2,1},{3,2},{4,7},{5,4},{6,5},{7,6},{8,11},{9,8},{10,9... | collective-permute-start | bytes 1179656 | tf_op jit(solution)/shard_map/ppermute | solution.py:19
  99.2 24.2 %collective-permute-start.24 = (bf16[96,4096]{1,0:T(8,128)(2,1)S(1)}, bf16[96,4096]{1,0:T(8,128)(2,1)S(1)}, u32[]{:S(2)}, u32[]{:S(2)}) collective-permute-start(bf16[96,4096]{1,0:T(8,128)(2,1)S(1)} %pad_maximum_fusion.2), channel_id=1, source_target_pairs={{0,1},{1,2},{2,3},{3,0},{4,5},{5,6},{6,7},{7,4},{8,9},{9,10},{10,1... | collective-permute-start | bytes 2359304 | tf_op jit(solution)/shard_map/ppermute | solution.py:19
  101.0 24.8 %collective-permute-start.26 = (bf16[96,4096]{1,0:T(8,128)(2,1)S(1)}, bf16[96,4096]{1,0:T(8,128)(2,1)S(1)}, u32[]{:S(2)}, u32[]{:S(2)}) collective-permute-start(bf16[96,4096]{1,0:T(8,128)(2,1)S(1)} %pad_maximum_fusion.3), channel_id=1, source_target_pairs={{0,3},{1,0},{2,1},{3,2},{4,7},{5,4},{6,5},{7,6},{8,11},{9,8},{10,9... | collective-permute-start | bytes 2359304 | tf_op jit(solution)/shard_map/ppermute | solution.py:19
  109.2 27.7 %collective-permute-start.13 = (bf16[96,4096]{1,0:T(8,128)(2,1)S(1)}, bf16[96,4096]{1,0:T(8,128)(2,1)S(1)}, u32[]{:S(2)}, u32[]{:S(2)}) collective-permute-start(bf16[96,4096]{1,0:T(8,128)(2,1)S(1)} %pad_maximum_fusion), channel_id=1, source_target_pairs={{0,1},{1,2},{2,3},{3,0},{4,5},{5,6},{6,7},{7,4},{8,9},{9,10},{10,1... | collective-permute-start | bytes 2359304 | tf_op jit(solution)/shard_map/ppermute | solution.py:19
  109.3 29.3 %collective-permute-start.15 = (bf16[96,4096]{1,0:T(8,128)(2,1)S(1)}, bf16[96,4096]{1,0:T(8,128)(2,1)S(1)}, u32[]{:S(2)}, u32[]{:S(2)}) collective-permute-start(bf16[96,4096]{1,0:T(8,128)(2,1)S(1)} %pad_maximum_fusion.1), channel_id=1, source_target_pairs={{0,3},{1,0},{2,1},{3,2},{4,7},{5,4},{6,5},{7,6},{8,11},{9,8},{10,9... | collective-permute-start | bytes 2359304 | tf_op jit(solution)/shard_map/ppermute | solution.py:19
  126.1 18.0 %copy-start.3 = (f32[1,2,64]{2,1,0:T(2,128)S(1)}, f32[1,2,64]{2,1,0:T(2,128)}, u32[]{:S(2)}) copy-start(f32[1,2,64]{2,1,0:T(2,128)} %param.8) | copy-start | bytes 1540
  126.1 17.8 %collective-permute-start.27 = (bf16[24,4096]{1,0:T(8,128)(2,1)S(1)}, bf16[24,4096]{1,0:T(8,128)(2,1)S(1)}, u32[]{:S(2)}, u32[]{:S(2)}) collective-permute-start(bf16[24,4096]{1,0:T(8,128)(2,1)S(1)} %get-tuple-element.37), channel_id=1, source_target_pairs={{0,12},{1,13},{2,14},{3,15},{4,0},{5,1},{6,2},{7,3},{8,4},{9,5},{1... | collective-permute-start | bytes 589832 | tf_op jit(solution)/shard_map/ppermute | solution.py:24
  129.4 14.6 %collective-permute-start.28 = (bf16[24,4096]{1,0:T(8,128)(2,1)S(1)}, bf16[24,4096]{1,0:T(8,128)(2,1)S(1)}, u32[]{:S(2)}, u32[]{:S(2)}) collective-permute-start(bf16[24,4096]{1,0:T(8,128)(2,1)S(1)} %get-tuple-element.36), channel_id=1, source_target_pairs={{0,8},{1,9},{2,10},{3,11},{4,12},{5,13},{6,14},{7,15},{8,0},{9,1},... | collective-permute-start | bytes 589832 | tf_op jit(solution)/shard_map/ppermute | solution.py:24
  130.5 13.5 %collective-permute-start.29 = (bf16[24,4096]{1,0:T(8,128)(2,1)S(1)}, bf16[24,4096]{1,0:T(8,128)(2,1)S(1)}, u32[]{:S(2)}, u32[]{:S(2)}) collective-permute-start(bf16[24,4096]{1,0:T(8,128)(2,1)S(1)} %get-tuple-element.35), channel_id=1, source_target_pairs={{0,4},{1,5},{2,6},{3,7},{4,8},{5,9},{6,10},{7,11},{8,12},{9,13},{1... | collective-permute-start | bytes 589832 | tf_op jit(solution)/shard_map/ppermute | solution.py:24
  139.0 8.6 %collective-permute-start.16 = (bf16[24,4096]{1,0:T(8,128)(2,1)S(1)}, bf16[24,4096]{1,0:T(8,128)(2,1)S(1)}, u32[]{:S(2)}, u32[]{:S(2)}) collective-permute-start(bf16[24,4096]{1,0:T(8,128)(2,1)S(1)} %get-tuple-element.41), channel_id=1, source_target_pairs={{0,12},{1,13},{2,14},{3,15},{4,0},{5,1},{6,2},{7,3},{8,4},{9,5},{1... | collective-permute-start | bytes 589832 | tf_op jit(solution)/shard_map/ppermute | solution.py:24
  142.3 7.3 %collective-permute-start.17 = (bf16[24,4096]{1,0:T(8,128)(2,1)S(1)}, bf16[24,4096]{1,0:T(8,128)(2,1)S(1)}, u32[]{:S(2)}, u32[]{:S(2)}) collective-permute-start(bf16[24,4096]{1,0:T(8,128)(2,1)S(1)} %get-tuple-element.40), channel_id=1, source_target_pairs={{0,8},{1,9},{2,10},{3,11},{4,12},{5,13},{6,14},{7,15},{8,0},{9,1},... | collective-permute-start | bytes 589832 | tf_op jit(solution)/shard_map/ppermute | solution.py:24
  143.9 7.6 %collective-permute-start.18 = (bf16[24,4096]{1,0:T(8,128)(2,1)S(1)}, bf16[24,4096]{1,0:T(8,128)(2,1)S(1)}, u32[]{:S(2)}, u32[]{:S(2)}) collective-permute-start(bf16[24,4096]{1,0:T(8,128)(2,1)S(1)} %get-tuple-element.39), channel_id=1, source_target_pairs={{0,4},{1,5},{2,6},{3,7},{4,8},{5,9},{6,10},{7,11},{8,12},{9,13},{1... | collective-permute-start | bytes 589832 | tf_op jit(solution)/shard_map/ppermute | solution.py:24

commit v3 on v2

--- a/solution.py
+++ b/solution.py
@@ -6,6 +6,7 @@
 from jax.sharding import PartitionSpec as P
 
 SIDE = 4
+BACK = ((4096,), (4096,))
 F32, BF16 = jnp.float32, jnp.bfloat16
 
 
@@ -31,15 +32,25 @@
     return [block, left, *far, right]
 
 
-def scatter_sum_x(parts):
+def scatter_sum_x(parts, sizes):
     half = parts[0].shape[0] // 2
     add = lambda a, b: (a.astype(F32) + b.astype(F32)).astype(BF16)
     to_right = shift_x(parts[2][:half], 1)
     to_left = shift_x(parts[2][half:], -1)
-    right = jnp.concatenate([add(parts[3][:half], to_right), parts[3][half:]], 0)
-    left = jnp.concatenate([parts[1][:half], add(parts[1][half:], to_left)], 0)
-    from_left, from_right = shift_x(right, 1), shift_x(left, -1)
-    return parts[0].astype(F32) + from_left.astype(F32) + from_right.astype(F32)
+    sums, start = [], 0
+    for c in sizes:
+        cols = slice(start, start + c)
+        start += c
+        right = jnp.concatenate(
+            [add(parts[3][:half, cols], to_right[:, cols]), parts[3][half:, cols]], 0
+        )
+        left = jnp.concatenate(
+            [parts[1][:half, cols], add(parts[1][half:, cols], to_left[:, cols])], 0
+        )
+        from_left, from_right = shift_x(right, 1), shift_x(left, -1)
+        total = parts[0][:, cols].astype(F32) + from_left.astype(F32) + from_right.astype(F32)
+        sums.append(total.astype(BF16))
+    return sums
 
 
 def slot_map(ids, row, cap):
@@ -99,33 +110,32 @@
     )(row, rows, gain, routing, *after)
 
 
-def finish(raw, batch, gate, onehot, back, earlier):
+def finish(raw, batch, batches, gate, onehot, back, span, earlier):
     toks, width = raw.shape[1:]
+    cols = back[0].shape[1]
 
     def kernel(r, g, s, *rest):
-        out = rest[-1]
         i, j = (lax.broadcasted_iota(jnp.int32, (toks, toks), d) for d in range(2))
         scale = jnp.sum(jnp.where(i == j, g[batch : batch + 1], 0.0), 1, keepdims=True)
-        if earlier:
-            out[:batch] = rest[SIDE][...]
         sums = sum(
             lax.dot_general(
                 s[k], rest[k][...], (((0,), (0,)), ((), ())), preferred_element_type=F32
             )
             for k in range(SIDE)
         )
-        out[batch] = (r[0].astype(F32) + scale * sums).astype(BF16)
+        rest[-1][0] = (r[0].astype(F32) + scale * sums).astype(BF16)
 
-    shape = (batch + 1, toks, width)
     return pl.pallas_call(
         kernel,
         grid=(1,),
-        out_shape=jax.ShapeDtypeStruct(shape, BF16),
+        out_shape=jax.ShapeDtypeStruct((batches, toks, width), BF16),
         in_specs=[
-            batch_of(raw.shape, 0),
-            *[whole(v.shape) for v in (gate, onehot, *back, *earlier)],
+            pl.BlockSpec((1, toks, cols), lambda i: (0, 0, span)),
+            *[whole(v.shape) for v in (gate, onehot, *back)],
+            *[pl.BlockSpec(memory_space=pl.ANY) for _ in earlier],
         ],
-        out_specs=whole(shape),
+        out_specs=pl.BlockSpec((1, toks, cols), lambda i: (batch, 0, span)),
+        input_output_aliases={3 + SIDE: 0} if earlier else {},
         compiler_params=pltpu.CompilerParams(vmem_limit_bytes=16 << 20),
         name="finish",
     )(raw, gate, onehot, *back, *earlier)
@@ -150,16 +160,21 @@
         both = jnp.einsum("rd,dkf->rkf", rows, w_gate_up[0, 0], preferred_element_type=F32)
         hidden.append((jax.nn.silu(both[:, 0]) * both[:, 1]).astype(BF16))
 
-    out = []
     for b in range(batches):
         part = jnp.dot(hidden[b], w_down[0, 0], preferred_element_type=F32).astype(BF16)
         part = part.reshape(SIDE, SIDE * cap, width)
-        summed = scatter_sum_x([part[j] for j in range(SIDE)]).astype(BF16)
-        summed = summed.reshape(SIDE, cap, width)
-        back = [summed[0]] + [shift_y(summed[k], -k) for k in range(1, SIDE)]
         onehot = slot_map(ids[b], row, cap).reshape(SIDE, cap, toks)
-        out = [finish(arriving[b], b, gates[0], onehot, back, out)]
-    return out[0][None]
+        summed = scatter_sum_x([part[j] for j in range(SIDE)], BACK[b])
+        total = summed[0].reshape(SIDE, cap, width)
+        back = [total[0]] + [shift_y(total[k], -k) for k in range(1, SIDE)]
+        if b == 0:
+            out = finish(arriving[b], b, batches, gates[0], onehot, back, 0, [])
+        else:
+            from_slots = slot_map(ids[b], row, cap).T
+            sums = jnp.dot(from_slots, jnp.concatenate(back, 0), preferred_element_type=F32)
+            done = arriving[b].astype(F32) + gates[0, b][None, :, None] * sums[None]
+            out = lax.dynamic_update_slice(out, done.astype(BF16), (b, 0, 0))
+    return out[None]
 
 
 def solution(mesh):

time: 155 us -> 152 us (0.981)
  waiting for transfers between devices: 88.5 us -> 81.9 us
  starting transfers between devices: 42.1 us -> 45.1 us
  matrix products: 9.08 us -> 11.3 us
  Pallas kernels: 7.91 us -> 5.97 us
    ppermute x12, waiting for transfers between devices: 16.6 us -> 13.2 us  [shift_y(): return lax.ppermute(v, 'et', [(i, (i + SIDE * by) % n) for i in range(n)])]
    ppermute x16, waiting for transfers between devices: 57.7 us -> 55.2 us  [shift_x(): return lax.ppermute(v, 'et', pairs)]
    ppermute x16, starting transfers between devices: 17.5 us -> 19.9 us  [shift_x(): return lax.ppermute(v, 'et', pairs)]
    dot_general x0 -> x1, matrix products: none -> 2.19 us  [per_device(): jnp.dot(from_slots, jnp.concatenate(back, 0), preferred_element_type=F32)]
    pallas_call x2 -> x1, Pallas kernels: 4.5 us -> 2.57 us  [finish(): pl.pallas_call(kernel, grid=(1,), out_shape=jax.ShapeDtypeStruct((batches...]
  transfers between devices with their start and end apart: 30 -> 30, of which waited for: 21 -> 17; matrix products, arithmetic and copies ran while one was open for 8% -> 9% of each run, Pallas kernels for 3% -> 4%
where the time goes in v3:
time: 152 us
  waiting for transfers between devices  81.9 us (54%)
  starting transfers between devices  45.1 us (30%)
  matrix products  11.3 us (7%)
  Pallas kernels  5.97 us (4%)
  local copies, waits for them, and re-layouts  4.19 us (3%)
  other arithmetic  2.82 us (2%)
    ppermute x16, waiting for transfers between devices, shift_x(): return lax.ppermute(v, 'et', pairs)  55.2 us
    ppermute x12, starting transfers between devices, shift_y(): return lax.ppermute(v, 'et', [(i, (i + SIDE * by) % n) for i in range(n)])  21.3 us
    ppermute x16, starting transfers between devices, shift_x(): return lax.ppermute(v, 'et', pairs)  19.9 us
    ppermute x2, waiting for transfers between devices, shift_z(): return lax.ppermute(v, 'section', [(i, (i + by) % n) for i in range(n)])  13.5 us
    ppermute x12, waiting for transfers between devices, shift_y(): return lax.ppermute(v, 'et', [(i, (i + SIDE * by) % n) for i in range(n)])  13.2 us
    dot_general x2, matrix products, per_device(): jnp.einsum('rd,dkf->rkf', rows, w_gate_up[0, 0], preferred_element_type=F32)  5.46 us
    ppermute x2, starting transfers between devices, shift_z(): return lax.ppermute(v, 'section', [(i, (i + by) % n) for i in range(n)])  3.83 us
    dot_general x2, matrix products, per_device(): jnp.dot(hidden[b], w_down[0, 0], preferred_element_type=F32).astype(BF16)  3.69 us
  transfers between devices with their start and end apart: 30, of which 17 were waited for; matrix products, arithmetic and copies ran while one was open for 9% of the time, Pallas kernels for 4%

profile of v3, /device:TPU:6, one launch (start us, length us, event | category | flops | bytes accessed | tf_op | source)
XLA Modules:
  0.0 151.7 jit_solution(5496569854772375721)
XLA Ops:
  0.0 2.5 %slice_bitcast_fusion = (bf16[1,64,4096]{2,1,0:T(8,128)(2,1)}, bf16[1,64,4096]{2,1,0:T(8,128)(2,1)}) fusion(bf16[1,2,64,4096]{3,2,1,0:T(8,128)(2,1)} %param.6), kind=kLoop, calls=%fused_computation.36 | loop fusion | bytes 2097152 | tf_op jit(solution)/shard_map/squeeze | solution.py:149
  2.5 1.9 %collective-permute-start = (bf16[1,64,4096]{2,1,0:T(8,128)(2,1)}, bf16[1,64,4096]{2,1,0:T(8,128)(2,1)}, u32[]{:S(2)}, u32[]{:S(2)}) collective-permute-start(bf16[1,64,4096]{2,1,0:T(8,128)(2,1)} %get-tuple-element.34), channel_id=1, source_target_pairs={{0,16},{16,32},{32,48},{48,64},{64,80},{80,96},{96,112},{112,0},{1... | collective-permute-start | bytes 1572872 | tf_op jit(solution)/shard_map/ppermute | solution.py:15
  4.4 1.9 %collective-permute-start.15 = (bf16[1,64,4096]{2,1,0:T(8,128)(2,1)}, bf16[1,64,4096]{2,1,0:T(8,128)(2,1)}, u32[]{:S(2)}, u32[]{:S(2)}) collective-permute-start(bf16[1,64,4096]{2,1,0:T(8,128)(2,1)} %get-tuple-element.33), channel_id=1, source_target_pairs={{0,16},{16,32},{32,48},{48,64},{64,80},{80,96},{96,112},{112,0},{1... | collective-permute-start | bytes 1572872 | tf_op jit(solution)/shard_map/ppermute | solution.py:15
  7.8 13.5 %collective-permute-done.a.r = bf16[1,64,4096]{2,1,0:T(8,128)(2,1)} collective-permute-done((bf16[1,64,4096]{2,1,0:T(8,128)(2,1)}, bf16[1,64,4096]{2,1,0:T(8,128)(2,1)}, u32[]{:S(2)}, u32[]{:S(2)}) %collective-permute-start) | collective-permute-done | bytes 524320 | tf_op jit(solution)/shard_map/ppermute | solution.py:15
  21.4 0.7 copy-done.1
  22.1 1.6 %pack.2 = (bf16[24,4096]{1,0:T(8,128)(2,1)S(1)}, bf16[24,4096]{1,0:T(8,128)(2,1)S(1)}, bf16[24,4096]{1,0:T(8,128)(2,1)S(1)}, bf16[24,4096]{1,0:T(8,128)(2,1)S(1)}) custom-call(s32[1]{0:T(128)} %bitcast.3.base, bf16[1,64,4096]{2,1,0:T(8,128)(2,1)} %collective-permute-done.a.r, f32[1,4096]{1,0:T(1,128)S(1)} %copy-done.1, f32[1,64]{1,0:T(1,128)S(1)} %get-tuple-element.62.r), custom_call_target="tpu_custom_call" | custom-call | tf_op jit(solution)/shard_map/pack/pallas_call | solution.py:96
  23.7 1.6 %collective-permute-start.1 = (bf16[24,4096]{1,0:T(8,128)(2,1)S(1)}, bf16[24,4096]{1,0:T(8,128)(2,1)S(1)}, u32[]{:S(2)}, u32[]{:S(2)}) collective-permute-start(bf16[24,4096]{1,0:T(8,128)(2,1)S(1)} %get-tuple-element.14), channel_id=1, source_target_pairs={{0,4},{1,5},{2,6},{3,7},{4,8},{5,9},{6,10},{7,11},{8,12},{9,13},{1... | collective-permute-start | bytes 589832 | tf_op jit(solution)/shard_map/ppermute | solution.py:25
  25.4 3.0 %collective-permute-start.2 = (bf16[24,4096]{1,0:T(8,128)(2,1)S(1)}, bf16[24,4096]{1,0:T(8,128)(2,1)S(1)}, u32[]{:S(2)}, u32[]{:S(2)}) collective-permute-start(bf16[24,4096]{1,0:T(8,128)(2,1)S(1)} %get-tuple-element.15), channel_id=1, source_target_pairs={{0,8},{1,9},{2,10},{3,11},{4,12},{5,13},{6,14},{7,15},{8,0},{9,1},... | collective-permute-start | bytes 589832 | tf_op jit(solution)/shard_map/ppermute | solution.py:25
  28.4 1.3 collective-permute-start.3
  29.8 2.7 %collective-permute-done.1 = bf16[24,4096]{1,0:T(8,128)(2,1)S(1)} collective-permute-done((bf16[24,4096]{1,0:T(8,128)(2,1)S(1)}, bf16[24,4096]{1,0:T(8,128)(2,1)S(1)}, u32[]{:S(2)}, u32[]{:S(2)}) %collective-permute-start.1) | collective-permute-done | bytes 196640 | tf_op jit(solution)/shard_map/ppermute | solution.py:25
  32.5 3.3 %collective-permute-done.2 = bf16[24,4096]{1,0:T(8,128)(2,1)S(1)} collective-permute-done((bf16[24,4096]{1,0:T(8,128)(2,1)S(1)}, bf16[24,4096]{1,0:T(8,128)(2,1)S(1)}, u32[]{:S(2)}, u32[]{:S(2)}) %collective-permute-start.2) | collective-permute-done | bytes 196640 | tf_op jit(solution)/shard_map/ppermute | solution.py:25
  36.4 1.6 %collective-permute-start.6 = (bf16[96,4096]{1,0:T(8,128)(2,1)S(1)}, bf16[96,4096]{1,0:T(8,128)(2,1)S(1)}, u32[]{:S(2)}, u32[]{:S(2)}) collective-permute-start(bf16[96,4096]{1,0:T(8,128)(2,1)S(1)} %get-tuple-element.51.rest_0_), channel_id=1, source_target_pairs={{0,3},{1,0},{2,1},{3,2},{4,7},{5,4},{6,5},{7,6},{8,11},{9,8},{10,9... | collective-permute-start | bytes 2359304 | tf_op jit(solution)/shard_map/ppermute | solution.py:20
  37.9 1.8 %pack.3 = (bf16[24,4096]{1,0:T(8,128)(2,1)S(1)}, bf16[24,4096]{1,0:T(8,128)(2,1)S(1)}, bf16[24,4096]{1,0:T(8,128)(2,1)S(1)}, bf16[24,4096]{1,0:T(8,128)(2,1)S(1)}) custom-call(s32[1]{0:T(128)} %bitcast.3.base, bf16[1,64,4096]{2,1,0:T(8,128)(2,1)} %collective-permute-done.15.a, f32[1,4096]{1,0:T(1,128)S(1)} %copy-done.2, f32[1,64]{1,0:T(1,128)S(1)} %get-tuple-element.63.r, ...), custom_call_target="tpu_custom_call" | custom-call | tf_op jit(solution)/shard_map/pack/pallas_call | solution.py:96
  39.7 1.3 collective-permute-start.16
  41.0 2.5 %collective-permute-start.17 = (bf16[24,4096]{1,0:T(8,128)(2,1)S(1)}, bf16[24,4096]{1,0:T(8,128)(2,1)S(1)}, u32[]{:S(2)}, u32[]{:S(2)}) collective-permute-start(bf16[24,4096]{1,0:T(8,128)(2,1)S(1)} %get-tuple-element.19), channel_id=1, source_target_pairs={{0,8},{1,9},{2,10},{3,11},{4,12},{5,13},{6,14},{7,15},{8,0},{9,1},... | collective-permute-start | bytes 589832 | tf_op jit(solution)/shard_map/ppermute | solution.py:25
  43.5 1.7 %collective-permute-start.18 = (bf16[24,4096]{1,0:T(8,128)(2,1)S(1)}, bf16[24,4096]{1,0:T(8,128)(2,1)S(1)}, u32[]{:S(2)}, u32[]{:S(2)}) collective-permute-start(bf16[24,4096]{1,0:T(8,128)(2,1)S(1)} %get-tuple-element.20), channel_id=1, source_target_pairs={{0,12},{1,13},{2,14},{3,15},{4,0},{5,1},{6,2},{7,3},{8,4},{9,5},{1... | collective-permute-start | bytes 589832 | tf_op jit(solution)/shard_map/ppermute | solution.py:25
  45.2 2.8 %collective-permute-done.16 = bf16[24,4096]{1,0:T(8,128)(2,1)S(1)} collective-permute-done((bf16[24,4096]{1,0:T(8,128)(2,1)S(1)}, bf16[24,4096]{1,0:T(8,128)(2,1)S(1)}, u32[]{:S(2)}, u32[]{:S(2)}) %collective-permute-start.16) | collective-permute-done | bytes 196640 | tf_op jit(solution)/shard_map/ppermute | solution.py:25
  48.0 2.1 %collective-permute-done.17 = bf16[24,4096]{1,0:T(8,128)(2,1)S(1)} collective-permute-done((bf16[24,4096]{1,0:T(8,128)(2,1)S(1)}, bf16[24,4096]{1,0:T(8,128)(2,1)S(1)}, u32[]{:S(2)}, u32[]{:S(2)}) %collective-permute-start.17) | collective-permute-done | bytes 196640 | tf_op jit(solution)/shard_map/ppermute | solution.py:25
  50.2 1.8 %collective-permute-start.19 = (bf16[96,4096]{1,0:T(8,128)(2,1)S(1)}, bf16[96,4096]{1,0:T(8,128)(2,1)S(1)}, u32[]{:S(2)}, u32[]{:S(2)}) collective-permute-start(bf16[96,4096]{1,0:T(8,128)(2,1)S(1)} %get-tuple-element.43), channel_id=1, source_target_pairs={{0,1},{1,2},{2,3},{3,0},{4,5},{5,6},{6,7},{7,4},{8,9},{9,10},{10,1... | collective-permute-start | bytes 2359304 | tf_op jit(solution)/shard_map/ppermute | solution.py:20
  52.4 3.4 %collective-permute-done.4 = bf16[96,4096]{1,0:T(8,128)(2,1)S(1)} collective-permute-done((bf16[96,4096]{1,0:T(8,128)(2,1)S(1)}, bf16[96,4096]{1,0:T(8,128)(2,1)S(1)}, u32[]{:S(2)}, u32[]{:S(2)}) %collective-permute-start.4) | collective-permute-done | bytes 786464 | tf_op jit(solution)/shard_map/ppermute | solution.py:20
  56.4 1.6 %collective-permute-start.7 = (bf16[48,4096]{1,0:T(8,128)(2,1)S(1)}, bf16[48,4096]{1,0:T(8,128)(2,1)S(1)}, u32[]{:S(2)}, u32[]{:S(2)}) collective-permute-start(bf16[48,4096]{1,0:T(8,128)(2,1)S(1)} %slice.185), channel_id=1, source_target_pairs={{0,3},{1,0},{2,1},{3,2},{4,7},{5,4},{6,5},{7,6},{8,11},{9,8},{10,9... | collective-permute-start | bytes 1179656 | tf_op jit(solution)/shard_map/ppermute | solution.py:20
  58.1 14.5 %collective-permute-done.19 = bf16[96,4096]{1,0:T(8,128)(2,1)S(1)} collective-permute-done((bf16[96,4096]{1,0:T(8,128)(2,1)S(1)}, bf16[96,4096]{1,0:T(8,128)(2,1)S(1)}, u32[]{:S(2)}, u32[]{:S(2)}) %collective-permute-start.19) | collective-permute-done | bytes 786464 | tf_op jit(solution)/shard_map/ppermute | solution.py:20
  72.7 1.2 collective-permute-start.20
  73.9 1.1 collective-permute-start.22
  75.1 5.9 %collective-permute-done.5 = bf16[48,4096]{1,0:T(8,128)(2,1)S(1)} collective-permute-done((bf16[48,4096]{1,0:T(8,128)(2,1)S(1)}, bf16[48,4096]{1,0:T(8,128)(2,1)S(1)}, u32[]{:S(2)}, u32[]{:S(2)}) %collective-permute-start.5) | collective-permute-done | bytes 393248 | tf_op jit(solution)/shard_map/ppermute | solution.py:20
  81.1 0.9 collective-permute-done.7
  82.2 2.7 %fusion.2 = f32[384,2,384]{2,0,1:T(8,128)S(1)} fusion(bf16[4096,2,384]{2,1,0:T(2,128)(2,1)S(1)} %bitcast.55, bf16[384,4096]{1,0:T(8,128)(2,1)S(1)} %constant_dynamic-update-slice_fusion.4), kind=kOutput, calls=%fused_computation.4 | convolution fusion | flops 2415919104 | bytes 10616832 | tf_op jit(solution)/shard_map/rd,dkf->rkf/dot_general | solution.py:160
  84.9 1.8 %convolution_convert_fusion.1 = bf16[384,4096]{1,0:T(8,128)(2,1)S(1)} fusion(bf16[1,1,384,4096]{3,2,1,0:T(8,128)(2,1)S(1)} %copy-done, f32[384,2,384]{2,0,1:T(8,128)S(1)} %fusion.2), kind=kOutput, calls=%fused_computation.1 | convolution fusion | flops 1210417152 | bytes 7471104 | tf_op jit(solution)/shard_map/dot_general | solution.py:164
  87.6 1.4 collective-permute-start.10
  89.7 2.7 %fusion = f32[384,2,384]{2,0,1:T(8,128)S(1)} fusion(bf16[4096,2,384]{2,1,0:T(2,128)(2,1)S(1)} %bitcast.56, bf16[384,4096]{1,0:T(8,128)(2,1)S(1)} %constant_dynamic-update-slice_fusion.16), kind=kOutput, calls=%fused_computation.2 | convolution fusion | flops 2415919104 | bytes 10616832 | tf_op jit(solution)/shard_map/rd,dkf->rkf/dot_general | solution.py:160
  92.5 1.8 %convolution_convert_fusion = bf16[384,4096]{1,0:T(8,128)(2,1)S(1)} fusion(bf16[1,1,384,4096]{3,2,1,0:T(8,128)(2,1)S(1)} %copy-done, f32[384,2,384]{2,0,1:T(8,128)S(1)} %fusion), kind=kOutput, calls=%fused_computation | convolution fusion | flops 1210417152 | bytes 7471104 | tf_op jit(solution)/shard_map/dot_general | solution.py:164
  94.4 1.3 collective-permute-start.23
  95.7 0.8 collective-permute-start.25
  97.0 2.1 %collective-permute-done.10 = bf16[48,4096]{1,0:T(8,128)(2,1)S(1)} collective-permute-done((bf16[48,4096]{1,0:T(8,128)(2,1)S(1)}, bf16[48,4096]{1,0:T(8,128)(2,1)S(1)}, u32[]{:S(2)}, u32[]{:S(2)}) %collective-permute-start.10) | collective-permute-done | bytes 393248 | tf_op jit(solution)/shard_map/ppermute | solution.py:20
  99.9 3.1 %collective-permute-start.9 = (bf16[96,4096]{1,0:T(8,128)(2,1)S(1)}, bf16[96,4096]{1,0:T(8,128)(2,1)S(1)}, u32[]{:S(2)}, u32[]{:S(2)}) collective-permute-start(bf16[96,4096]{1,0:T(8,128)(2,1)S(1)} %pad_maximum_fusion), channel_id=1, source_target_pairs={{0,1},{1,2},{2,3},{3,0},{4,5},{5,6},{6,7},{7,4},{8,9},{9,10},{10,1... | collective-permute-start | bytes 2359304 | tf_op jit(solution)/shard_map/ppermute | solution.py:20
  103.0 3.6 %collective-permute-done.23 = bf16[48,4096]{1,0:T(8,128)(2,1)S(1)} collective-permute-done((bf16[48,4096]{1,0:T(8,128)(2,1)S(1)}, bf16[48,4096]{1,0:T(8,128)(2,1)S(1)}, u32[]{:S(2)}, u32[]{:S(2)}) %collective-permute-start.23) | collective-permute-done | bytes 393248 | tf_op jit(solution)/shard_map/ppermute | solution.py:20
  106.6 2.4 %collective-permute-done.25 = bf16[48,4096]{1,0:T(8,128)(2,1)S(1)} collective-permute-done((bf16[48,4096]{1,0:T(8,128)(2,1)S(1)}, bf16[48,4096]{1,0:T(8,128)(2,1)S(1)}, u32[]{:S(2)}, u32[]{:S(2)}) %collective-permute-start.25) | collective-permute-done | bytes 393248 | tf_op jit(solution)/shard_map/ppermute | solution.py:20
  109.4 3.3 %collective-permute-start.24 = (bf16[96,4096]{1,0:T(8,128)(2,1)S(1)}, bf16[96,4096]{1,0:T(8,128)(2,1)S(1)}, u32[]{:S(2)}, u32[]{:S(2)}) collective-permute-start(bf16[96,4096]{1,0:T(8,128)(2,1)S(1)} %pad_maximum_fusion.2), channel_id=1, source_target_pairs={{0,1},{1,2},{2,3},{3,0},{4,5},{5,6},{6,7},{7,4},{8,9},{9,10},{10,1... | collective-permute-start | bytes 2359304 | tf_op jit(solution)/shard_map/ppermute | solution.py:20
  112.7 13.1 %collective-permute-done.11 = bf16[96,4096]{1,0:T(8,128)(2,1)S(1)} collective-permute-done((bf16[96,4096]{1,0:T(8,128)(2,1)S(1)}, bf16[96,4096]{1,0:T(8,128)(2,1)S(1)}, u32[]{:S(2)}, u32[]{:S(2)}) %collective-permute-start.11) | collective-permute-done | bytes 786464 | tf_op jit(solution)/shard_map/ppermute | solution.py:20
  126.2 3.2 %collective-permute-start.12 = (bf16[24,4096]{1,0:T(8,128)(2,1)S(1)}, bf16[24,4096]{1,0:T(8,128)(2,1)S(1)}, u32[]{:S(2)}, u32[]{:S(2)}) collective-permute-start(bf16[24,4096]{1,0:T(8,128)(2,1)S(1)} %get-tuple-element.41), channel_id=1, source_target_pairs={{0,12},{1,13},{2,14},{3,15},{4,0},{5,1},{6,2},{7,3},{8,4},{9,5},{1... | collective-permute-start | bytes 589832 | tf_op jit(solution)/shard_map/ppermute | solution.py:25
  129.5 1.1 collective-permute-start.13
  130.6 8.1 %collective-permute-done.26 = bf16[96,4096]{1,0:T(8,128)(2,1)S(1)} collective-permute-done((bf16[96,4096]{1,0:T(8,128)(2,1)S(1)}, bf16[96,4096]{1,0:T(8,128)(2,1)S(1)}, u32[]{:S(2)}, u32[]{:S(2)}) %collective-permute-start.26) | collective-permute-done | bytes 786464 | tf_op jit(solution)/shard_map/ppermute | solution.py:20
  139.1 2.7 %collective-permute-start.29 = (bf16[24,4096]{1,0:T(8,128)(2,1)S(1)}, bf16[24,4096]{1,0:T(8,128)(2,1)S(1)}, u32[]{:S(2)}, u32[]{:S(2)}) collective-permute-start(bf16[24,4096]{1,0:T(8,128)(2,1)S(1)} %get-tuple-element.36), channel_id=1, source_target_pairs={{0,4},{1,5},{2,6},{3,7},{4,8},{5,9},{6,10},{7,11},{8,12},{9,13},{1... | collective-permute-start | bytes 589832 | tf_op jit(solution)/shard_map/ppermute | solution.py:25
  141.8 1.9 %collective-permute-start.28 = (bf16[24,4096]{1,0:T(8,128)(2,1)S(1)}, bf16[24,4096]{1,0:T(8,128)(2,1)S(1)}, u32[]{:S(2)}, u32[]{:S(2)}) collective-permute-start(bf16[24,4096]{1,0:T(8,128)(2,1)S(1)} %get-tuple-element.37), channel_id=1, source_target_pairs={{0,8},{1,9},{2,10},{3,11},{4,12},{5,13},{6,14},{7,15},{8,0},{9,1},... | collective-permute-start | bytes 589832 | tf_op jit(solution)/shard_map/ppermute | solution.py:25
  143.7 0.9 collective-permute-start.27
  144.6 2.6 %finish.1 = bf16[2,64,4096]{2,1,0:T(8,128)(2,1)} custom-call(bf16[1,64,4096]{2,1,0:T(8,128)(2,1)} %collective-permute-done.a.r, f32[2,64]{1,0:T(2,128)S(1)} %bitcast.51, bf16[4,24,64]{2,1,0:T(8,128)(2,1)S(1)} %compare_convert_fusion.s, bf16[24,4096]{1,0:T(8,128)(2,1)S(1)} %get-tuple-element.42.rest_0_, bf16[24,4096]{1,0:T(8,128)(2,1)S(1)} %collective-permute-done.12.rest_1_, ...), custom_call_target="tpu_custom_call" | custom-call | tf_op jit(solution)/shard_map/finish/pallas_call | solution.py:128
  147.2 2.3 %collective-permute-done.28 = bf16[24,4096]{1,0:T(8,128)(2,1)S(1)} collective-permute-done((bf16[24,4096]{1,0:T(8,128)(2,1)S(1)}, bf16[24,4096]{1,0:T(8,128)(2,1)S(1)}, u32[]{:S(2)}, u32[]{:S(2)}) %collective-permute-start.28) | collective-permute-done | bytes 196640 | tf_op jit(solution)/shard_map/ppermute | solution.py:25
  149.5 2.2 %fusion.15 = bf16[1,2,64,4096]{3,2,1,0:T(8,128)(2,1)} fusion(bf16[1,2,64,4096]{3,2,1,0:T(8,128)(2,1)} %bitcast.52, bf16[1,64,4096]{2,1,0:T(8,128)(2,1)} %collective-permute-done.15.a, bf16[24,4096]{1,0:T(8,128)(2,1)S(1)} %collective-permute-done.29, bf16[24,4096]{1,0:T(8,128)(2,1)S(1)} %collective-permute-done.28, ...), kind=kOutput, calls=%fused_computation.21 | convolution fusion | flops 54532096 | bytes 1835520 | tf_op jit(solution)/shard_map/dot_general | solution.py:174
  (72 shorter events, 7.6 us)
Async XLA Ops:
  0.0 84.9 %copy-start = (bf16[1,1,384,4096]{3,2,1,0:T(8,128)(2,1)S(1)}, bf16[1,1,384,4096]{3,2,1,0:T(8,128)(2,1)}, u32[]{:S(2)}) copy-start(bf16[1,1,384,4096]{3,2,1,0:T(8,128)(2,1)} %param.11) | copy-start | bytes 9437188
  0.0 37.9 %copy-start.2 = (f32[1,4096]{1,0:T(1,128)S(1)}, f32[1,4096]{1,0:T(1,128)}, u32[]{:S(2)}) copy-start(f32[1,4096]{1,0:T(1,128)} %g.3) | copy-start | bytes 49156
  2.5 18.9 %collective-permute-start = (bf16[1,64,4096]{2,1,0:T(8,128)(2,1)}, bf16[1,64,4096]{2,1,0:T(8,128)(2,1)}, u32[]{:S(2)}, u32[]{:S(2)}) collective-permute-start(bf16[1,64,4096]{2,1,0:T(8,128)(2,1)} %get-tuple-element.34), channel_id=1, source_target_pairs={{0,16},{16,32},{32,48},{48,64},{64,80},{80,96},{96,112},{112,0},{1... | collective-permute-start | bytes 1572872 | tf_op jit(solution)/shard_map/ppermute | solution.py:15
  4.4 33.5 %collective-permute-start.15 = (bf16[1,64,4096]{2,1,0:T(8,128)(2,1)}, bf16[1,64,4096]{2,1,0:T(8,128)(2,1)}, u32[]{:S(2)}, u32[]{:S(2)}) collective-permute-start(bf16[1,64,4096]{2,1,0:T(8,128)(2,1)} %get-tuple-element.33), channel_id=1, source_target_pairs={{0,16},{16,32},{32,48},{48,64},{64,80},{80,96},{96,112},{112,0},{1... | collective-permute-start | bytes 1572872 | tf_op jit(solution)/shard_map/ppermute | solution.py:15
  21.4 0.7 copy-start.1
  23.7 8.7 %collective-permute-start.1 = (bf16[24,4096]{1,0:T(8,128)(2,1)S(1)}, bf16[24,4096]{1,0:T(8,128)(2,1)S(1)}, u32[]{:S(2)}, u32[]{:S(2)}) collective-permute-start(bf16[24,4096]{1,0:T(8,128)(2,1)S(1)} %get-tuple-element.14), channel_id=1, source_target_pairs={{0,4},{1,5},{2,6},{3,7},{4,8},{5,9},{6,10},{7,11},{8,12},{9,13},{1... | collective-permute-start | bytes 589832 | tf_op jit(solution)/shard_map/ppermute | solution.py:25
  25.4 10.3 %collective-permute-start.2 = (bf16[24,4096]{1,0:T(8,128)(2,1)S(1)}, bf16[24,4096]{1,0:T(8,128)(2,1)S(1)}, u32[]{:S(2)}, u32[]{:S(2)}) collective-permute-start(bf16[24,4096]{1,0:T(8,128)(2,1)S(1)} %get-tuple-element.15), channel_id=1, source_target_pairs={{0,8},{1,9},{2,10},{3,11},{4,12},{5,13},{6,14},{7,15},{8,0},{9,1},... | collective-permute-start | bytes 589832 | tf_op jit(solution)/shard_map/ppermute | solution.py:25
  28.4 7.4 %collective-permute-start.3 = (bf16[24,4096]{1,0:T(8,128)(2,1)S(1)}, bf16[24,4096]{1,0:T(8,128)(2,1)S(1)}, u32[]{:S(2)}, u32[]{:S(2)}) collective-permute-start(bf16[24,4096]{1,0:T(8,128)(2,1)S(1)} %get-tuple-element.16), channel_id=1, source_target_pairs={{0,12},{1,13},{2,14},{3,15},{4,0},{5,1},{6,2},{7,3},{8,4},{9,5},{1... | collective-permute-start | bytes 589832 | tf_op jit(solution)/shard_map/ppermute | solution.py:25
  35.8 20.0 %collective-permute-start.4 = (bf16[96,4096]{1,0:T(8,128)(2,1)S(1)}, bf16[96,4096]{1,0:T(8,128)(2,1)S(1)}, u32[]{:S(2)}, u32[]{:S(2)}) collective-permute-start(bf16[96,4096]{1,0:T(8,128)(2,1)S(1)} %get-tuple-element.51.rest_0_), channel_id=1, source_target_pairs={{0,1},{1,2},{2,3},{3,0},{4,5},{5,6},{6,7},{7,4},{8,9},{9,10},{10,1... | collective-permute-start | bytes 2359304 | tf_op jit(solution)/shard_map/ppermute | solution.py:20
  36.4 20.0 %collective-permute-start.6 = (bf16[96,4096]{1,0:T(8,128)(2,1)S(1)}, bf16[96,4096]{1,0:T(8,128)(2,1)S(1)}, u32[]{:S(2)}, u32[]{:S(2)}) collective-permute-start(bf16[96,4096]{1,0:T(8,128)(2,1)S(1)} %get-tuple-element.51.rest_0_), channel_id=1, source_target_pairs={{0,3},{1,0},{2,1},{3,2},{4,7},{5,4},{6,5},{7,6},{8,11},{9,8},{10,9... | collective-permute-start | bytes 2359304 | tf_op jit(solution)/shard_map/ppermute | solution.py:20
  37.9 44.2 %slice-start = ((s8[6291456]{0:T(1024)(128)(4,1)}), s8[4194304]{0:T(1024)(128)(4,1)S(1)}, s32[]{:S(2)}) async-start(s8[6291456]{0:T(1024)(128)(4,1)} %bitcast.53), calls=%async_computation | async-start | bytes 8388608
  39.7 8.3 %collective-permute-start.16 = (bf16[24,4096]{1,0:T(8,128)(2,1)S(1)}, bf16[24,4096]{1,0:T(8,128)(2,1)S(1)}, u32[]{:S(2)}, u32[]{:S(2)}) collective-permute-start(bf16[24,4096]{1,0:T(8,128)(2,1)S(1)} %get-tuple-element.18), channel_id=1, source_target_pairs={{0,4},{1,5},{2,6},{3,7},{4,8},{5,9},{6,10},{7,11},{8,12},{9,13},{1... | collective-permute-start | bytes 589832 | tf_op jit(solution)/shard_map/ppermute | solution.py:25
  41.0 9.0 %collective-permute-start.17 = (bf16[24,4096]{1,0:T(8,128)(2,1)S(1)}, bf16[24,4096]{1,0:T(8,128)(2,1)S(1)}, u32[]{:S(2)}, u32[]{:S(2)}) collective-permute-start(bf16[24,4096]{1,0:T(8,128)(2,1)S(1)} %get-tuple-element.19), channel_id=1, source_target_pairs={{0,8},{1,9},{2,10},{3,11},{4,12},{5,13},{6,14},{7,15},{8,0},{9,1},... | collective-permute-start | bytes 589832 | tf_op jit(solution)/shard_map/ppermute | solution.py:25
  43.5 6.6 %collective-permute-start.18 = (bf16[24,4096]{1,0:T(8,128)(2,1)S(1)}, bf16[24,4096]{1,0:T(8,128)(2,1)S(1)}, u32[]{:S(2)}, u32[]{:S(2)}) collective-permute-start(bf16[24,4096]{1,0:T(8,128)(2,1)S(1)} %get-tuple-element.20), channel_id=1, source_target_pairs={{0,12},{1,13},{2,14},{3,15},{4,0},{5,1},{6,2},{7,3},{8,4},{9,5},{1... | collective-permute-start | bytes 589832 | tf_op jit(solution)/shard_map/ppermute | solution.py:25
  50.2 22.5 %collective-permute-start.19 = (bf16[96,4096]{1,0:T(8,128)(2,1)S(1)}, bf16[96,4096]{1,0:T(8,128)(2,1)S(1)}, u32[]{:S(2)}, u32[]{:S(2)}) collective-permute-start(bf16[96,4096]{1,0:T(8,128)(2,1)S(1)} %get-tuple-element.43), channel_id=1, source_target_pairs={{0,1},{1,2},{2,3},{3,0},{4,5},{5,6},{6,7},{7,4},{8,9},{9,10},{10,1... | collective-permute-start | bytes 2359304 | tf_op jit(solution)/shard_map/ppermute | solution.py:20
  51.9 22.0 %collective-permute-start.21 = (bf16[96,4096]{1,0:T(8,128)(2,1)S(1)}, bf16[96,4096]{1,0:T(8,128)(2,1)S(1)}, u32[]{:S(2)}, u32[]{:S(2)}) collective-permute-start(bf16[96,4096]{1,0:T(8,128)(2,1)S(1)} %get-tuple-element.43), channel_id=1, source_target_pairs={{0,3},{1,0},{2,1},{3,2},{4,7},{5,4},{6,5},{7,6},{8,11},{9,8},{10,9... | collective-permute-start | bytes 2359304 | tf_op jit(solution)/shard_map/ppermute | solution.py:20
  55.8 25.2 %collective-permute-start.5 = (bf16[48,4096]{1,0:T(8,128)(2,1)S(1)}, bf16[48,4096]{1,0:T(8,128)(2,1)S(1)}, u32[]{:S(2)}, u32[]{:S(2)}) collective-permute-start(bf16[48,4096]{1,0:T(8,128)(2,1)S(1)} %slice.184), channel_id=1, source_target_pairs={{0,1},{1,2},{2,3},{3,0},{4,5},{5,6},{6,7},{7,4},{8,9},{9,10},{10,1... | collective-permute-start | bytes 1179656 | tf_op jit(solution)/shard_map/ppermute | solution.py:20
  56.4 25.6 %collective-permute-start.7 = (bf16[48,4096]{1,0:T(8,128)(2,1)S(1)}, bf16[48,4096]{1,0:T(8,128)(2,1)S(1)}, u32[]{:S(2)}, u32[]{:S(2)}) collective-permute-start(bf16[48,4096]{1,0:T(8,128)(2,1)S(1)} %slice.185), channel_id=1, source_target_pairs={{0,3},{1,0},{2,1},{3,2},{4,7},{5,4},{6,5},{7,6},{8,11},{9,8},{10,9... | collective-permute-start | bytes 1179656 | tf_op jit(solution)/shard_map/ppermute | solution.py:20
  58.0 24.1 %slice-start.1 = ((s8[6291456]{0:T(1024)(128)(4,1)}), s8[2097152]{0:T(1024)(128)(4,1)S(1)}, s32[]{:S(2)}) async-start(s8[6291456]{0:T(1024)(128)(4,1)} %bitcast.53), calls=%async_computation.1 | async-start | bytes 4194304
  72.7 16.4 %collective-permute-start.20 = (bf16[48,4096]{1,0:T(8,128)(2,1)S(1)}, bf16[48,4096]{1,0:T(8,128)(2,1)S(1)}, u32[]{:S(2)}, u32[]{:S(2)}) collective-permute-start(bf16[48,4096]{1,0:T(8,128)(2,1)S(1)} %slice.199), channel_id=1, source_target_pairs={{0,1},{1,2},{2,3},{3,0},{4,5},{5,6},{6,7},{7,4},{8,9},{9,10},{10,1... | collective-permute-start | bytes 1179656 | tf_op jit(solution)/shard_map/ppermute | solution.py:20
  73.9 15.7 %collective-permute-start.22 = (bf16[48,4096]{1,0:T(8,128)(2,1)S(1)}, bf16[48,4096]{1,0:T(8,128)(2,1)S(1)}, u32[]{:S(2)}, u32[]{:S(2)}) collective-permute-start(bf16[48,4096]{1,0:T(8,128)(2,1)S(1)} %slice.200), channel_id=1, source_target_pairs={{0,3},{1,0},{2,1},{3,2},{4,7},{5,4},{6,5},{7,6},{8,11},{9,8},{10,9... | collective-permute-start | bytes 1179656 | tf_op jit(solution)/shard_map/ppermute | solution.py:20
  86.9 10.1 %collective-permute-start.8 = (bf16[48,4096]{1,0:T(8,128)(2,1)S(1)}, bf16[48,4096]{1,0:T(8,128)(2,1)S(1)}, u32[]{:S(2)}, u32[]{:S(2)}) collective-permute-start(bf16[48,4096]{1,0:T(8,128)(2,1)S(1)} %get-tuple-element.29), channel_id=1, source_target_pairs={{0,1},{1,2},{2,3},{3,0},{4,5},{5,6},{6,7},{7,4},{8,9},{9,10},{10,1... | collective-permute-start | bytes 1179656 | tf_op jit(solution)/shard_map/ppermute | solution.py:20
  87.6 11.5 %collective-permute-start.10 = (bf16[48,4096]{1,0:T(8,128)(2,1)S(1)}, bf16[48,4096]{1,0:T(8,128)(2,1)S(1)}, u32[]{:S(2)}, u32[]{:S(2)}) collective-permute-start(bf16[48,4096]{1,0:T(8,128)(2,1)S(1)} %get-tuple-element.30), channel_id=1, source_target_pairs={{0,3},{1,0},{2,1},{3,2},{4,7},{5,4},{6,5},{7,6},{8,11},{9,8},{10,9... | collective-permute-start | bytes 1179656 | tf_op jit(solution)/shard_map/ppermute | solution.py:20
  94.4 12.1 %collective-permute-start.23 = (bf16[48,4096]{1,0:T(8,128)(2,1)S(1)}, bf16[48,4096]{1,0:T(8,128)(2,1)S(1)}, u32[]{:S(2)}, u32[]{:S(2)}) collective-permute-start(bf16[48,4096]{1,0:T(8,128)(2,1)S(1)} %get-tuple-element.23), channel_id=1, source_target_pairs={{0,1},{1,2},{2,3},{3,0},{4,5},{5,6},{6,7},{7,4},{8,9},{9,10},{10,1... | collective-permute-start | bytes 1179656 | tf_op jit(solution)/shard_map/ppermute | solution.py:20
  95.7 13.3 %collective-permute-start.25 = (bf16[48,4096]{1,0:T(8,128)(2,1)S(1)}, bf16[48,4096]{1,0:T(8,128)(2,1)S(1)}, u32[]{:S(2)}, u32[]{:S(2)}) collective-permute-start(bf16[48,4096]{1,0:T(8,128)(2,1)S(1)} %get-tuple-element.24), channel_id=1, source_target_pairs={{0,3},{1,0},{2,1},{3,2},{4,7},{5,4},{6,5},{7,6},{8,11},{9,8},{10,9... | collective-permute-start | bytes 1179656 | tf_op jit(solution)/shard_map/ppermute | solution.py:20
  99.3 26.5 %collective-permute-start.11 = (bf16[96,4096]{1,0:T(8,128)(2,1)S(1)}, bf16[96,4096]{1,0:T(8,128)(2,1)S(1)}, u32[]{:S(2)}, u32[]{:S(2)}) collective-permute-start(bf16[96,4096]{1,0:T(8,128)(2,1)S(1)} %pad_maximum_fusion.1), channel_id=1, source_target_pairs={{0,3},{1,0},{2,1},{3,2},{4,7},{5,4},{6,5},{7,6},{8,11},{9,8},{10,9... | collective-permute-start | bytes 2359304 | tf_op jit(solution)/shard_map/ppermute | solution.py:20
  99.9 26.0 %collective-permute-start.9 = (bf16[96,4096]{1,0:T(8,128)(2,1)S(1)}, bf16[96,4096]{1,0:T(8,128)(2,1)S(1)}, u32[]{:S(2)}, u32[]{:S(2)}) collective-permute-start(bf16[96,4096]{1,0:T(8,128)(2,1)S(1)} %pad_maximum_fusion), channel_id=1, source_target_pairs={{0,1},{1,2},{2,3},{3,0},{4,5},{5,6},{6,7},{7,4},{8,9},{9,10},{10,1... | collective-permute-start | bytes 2359304 | tf_op jit(solution)/shard_map/ppermute | solution.py:20
  109.3 29.4 %collective-permute-start.26 = (bf16[96,4096]{1,0:T(8,128)(2,1)S(1)}, bf16[96,4096]{1,0:T(8,128)(2,1)S(1)}, u32[]{:S(2)}, u32[]{:S(2)}) collective-permute-start(bf16[96,4096]{1,0:T(8,128)(2,1)S(1)} %pad_maximum_fusion.3), channel_id=1, source_target_pairs={{0,3},{1,0},{2,1},{3,2},{4,7},{5,4},{6,5},{7,6},{8,11},{9,8},{10,9... | collective-permute-start | bytes 2359304 | tf_op jit(solution)/shard_map/ppermute | solution.py:20
  109.4 29.3 %collective-permute-start.24 = (bf16[96,4096]{1,0:T(8,128)(2,1)S(1)}, bf16[96,4096]{1,0:T(8,128)(2,1)S(1)}, u32[]{:S(2)}, u32[]{:S(2)}) collective-permute-start(bf16[96,4096]{1,0:T(8,128)(2,1)S(1)} %pad_maximum_fusion.2), channel_id=1, source_target_pairs={{0,1},{1,2},{2,3},{3,0},{4,5},{5,6},{6,7},{7,4},{8,9},{9,10},{10,1... | collective-permute-start | bytes 2359304 | tf_op jit(solution)/shard_map/ppermute | solution.py:20
  126.2 18.4 %copy-start.3 = (f32[1,2,64]{2,1,0:T(2,128)S(1)}, f32[1,2,64]{2,1,0:T(2,128)}, u32[]{:S(2)}) copy-start(f32[1,2,64]{2,1,0:T(2,128)} %param.8) | copy-start | bytes 1540
  126.2 17.5 %collective-permute-start.12 = (bf16[24,4096]{1,0:T(8,128)(2,1)S(1)}, bf16[24,4096]{1,0:T(8,128)(2,1)S(1)}, u32[]{:S(2)}, u32[]{:S(2)}) collective-permute-start(bf16[24,4096]{1,0:T(8,128)(2,1)S(1)} %get-tuple-element.41), channel_id=1, source_target_pairs={{0,12},{1,13},{2,14},{3,15},{4,0},{5,1},{6,2},{7,3},{8,4},{9,5},{1... | collective-permute-start | bytes 589832 | tf_op jit(solution)/shard_map/ppermute | solution.py:25
  129.5 15.1 %collective-permute-start.13 = (bf16[24,4096]{1,0:T(8,128)(2,1)S(1)}, bf16[24,4096]{1,0:T(8,128)(2,1)S(1)}, u32[]{:S(2)}, u32[]{:S(2)}) collective-permute-start(bf16[24,4096]{1,0:T(8,128)(2,1)S(1)} %get-tuple-element.40), channel_id=1, source_target_pairs={{0,8},{1,9},{2,10},{3,11},{4,12},{5,13},{6,14},{7,15},{8,0},{9,1},... | collective-permute-start | bytes 589832 | tf_op jit(solution)/shard_map/ppermute | solution.py:25
  130.6 14.0 %collective-permute-start.14 = (bf16[24,4096]{1,0:T(8,128)(2,1)S(1)}, bf16[24,4096]{1,0:T(8,128)(2,1)S(1)}, u32[]{:S(2)}, u32[]{:S(2)}) collective-permute-start(bf16[24,4096]{1,0:T(8,128)(2,1)S(1)} %get-tuple-element.39), channel_id=1, source_target_pairs={{0,4},{1,5},{2,6},{3,7},{4,8},{5,9},{6,10},{7,11},{8,12},{9,13},{1... | collective-permute-start | bytes 589832 | tf_op jit(solution)/shard_map/ppermute | solution.py:25
  139.1 8.1 %collective-permute-start.29 = (bf16[24,4096]{1,0:T(8,128)(2,1)S(1)}, bf16[24,4096]{1,0:T(8,128)(2,1)S(1)}, u32[]{:S(2)}, u32[]{:S(2)}) collective-permute-start(bf16[24,4096]{1,0:T(8,128)(2,1)S(1)} %get-tuple-element.36), channel_id=1, source_target_pairs={{0,4},{1,5},{2,6},{3,7},{4,8},{5,9},{6,10},{7,11},{8,12},{9,13},{1... | collective-permute-start | bytes 589832 | tf_op jit(solution)/shard_map/ppermute | solution.py:25
  141.8 7.7 %collective-permute-start.28 = (bf16[24,4096]{1,0:T(8,128)(2,1)S(1)}, bf16[24,4096]{1,0:T(8,128)(2,1)S(1)}, u32[]{:S(2)}, u32[]{:S(2)}) collective-permute-start(bf16[24,4096]{1,0:T(8,128)(2,1)S(1)} %get-tuple-element.37), channel_id=1, source_target_pairs={{0,8},{1,9},{2,10},{3,11},{4,12},{5,13},{6,14},{7,15},{8,0},{9,1},... | collective-permute-start | bytes 589832 | tf_op jit(solution)/shard_map/ppermute | solution.py:25
  143.7 5.8 %collective-permute-start.27 = (bf16[24,4096]{1,0:T(8,128)(2,1)S(1)}, bf16[24,4096]{1,0:T(8,128)(2,1)S(1)}, u32[]{:S(2)}, u32[]{:S(2)}) collective-permute-start(bf16[24,4096]{1,0:T(8,128)(2,1)S(1)} %get-tuple-element.38), channel_id=1, source_target_pairs={{0,12},{1,13},{2,14},{3,15},{4,0},{5,1},{6,2},{7,3},{8,4},{9,5},{1... | collective-permute-start | bytes 589832 | tf_op jit(solution)/shard_map/ppermute | solution.py:25
